TPU v7x, 128 devices: a whole 4x4x4 slice. The times are simulated.
128 devices in a mesh: blk: 16 (over z, y), rows: 8 (over x, core).
Axes of the slice: x: 4, y: 4, z: 4, core: 2. Of those that a mesh axis runs over, the one named last changes fastest.
Arguments:
- fine_blocks: bfloat16 [8, 16, 16, 8, 128, 128], P('rows', 'blk'), may hold values from -0.5 to 0.5
- block_rows: int32 [8, 16, 16, 8], P('rows', 'blk'), may hold values from 0 to 15
- block_cols: int32 [8, 16, 16, 8], P('rows', 'blk'), may hold values from 0 to 15
- block_counts: int32 [8, 16, 16], P('rows', 'blk'), may hold values from 1 to 8, 72 in all within a row
- prolong_blocks: bfloat16 [8, 256, 128, 384], P('rows', 'blk'), may hold values from -1.1953125 to 1.1953125
- prolong_mask: int32 [8, 256, 3], P('rows', 'blk'), may hold values 0 or 1
Outputs:
- coarse_blocks: float32 [8, 16, 128, 16, 5, 128], P('rows', 'blk')
Inputs may be any that keep to these rules, and one draw needn't show every extreme that they name: `block_counts`: the 16 counts of one device sum to 72, and one of them is 8.
All inputs are finite; a program needn't handle non-finite values. No bound on the sum of `prolong_mask` on one device may be relied on, other than what follows from the above.
Results may differ from a plain program's by a relative error of at most 0.004.
Values may be sent and summed in bfloat16 or wider, within the bound.
A program may use at most 128 MiB of HBM per device.

v0:
```python
import jax
import jax.numpy as jnp
from jax import lax
from jax.sharding import PartitionSpec as P


def padded_2(array, sides, width):
    for axis, dim in sides:
        size, length = (lax.axis_size(axis), array.shape[dim])
        up = [(i, (i + 1) % size) for i in range(size - 1)]
        down = [(j, i) for i, j in up]
        last = lax.slice_in_dim(array, length - width, length, axis=dim)
        initial = lax.slice_in_dim(array, 0, width, axis=dim)
        before = lax.ppermute(last, axis, up)
        after = lax.ppermute(initial, axis, down)
        array = jnp.concatenate([before, array, after], axis=dim)
    return array


def per_device(fine_blocks, block_rows, block_cols, block_counts, prolong_blocks, prolong_mask):
    matrix = fine_blocks[0, 0]
    slot_rows = block_rows[0, 0]
    slot_cols = block_cols[0, 0]
    slot_counts = block_counts[0, 0]
    prolong = prolong_blocks[0]
    pattern = prolong_mask[0]
    shard_rows, pore_count, prolong_width = prolong.shape
    coarse_width = prolong_width // 3
    slot_total = matrix.shape[1]
    panels = lax.axis_size("blk")
    groups = lax.axis_size("rows")
    group_index = lax.axis_index("rows")
    offsets = group_index + jnp.arange(3, dtype=jnp.int32) - 1
    keeper = (pattern == 1) & (offsets[None, :] >= 0) & (offsets[None, :] < groups)
    masked = (
        prolong.reshape(shard_rows, pore_count, 3, coarse_width)
        * keeper[:, None, :, None].astype(jnp.bfloat16)
    ).reshape(shard_rows, pore_count, prolong_width)
    row_ids = jnp.arange(shard_rows, dtype=jnp.int32)
    slot_ids = jnp.arange(slot_total, dtype=jnp.int32)

    def row_products(peer_index, panel_rows):
        local_block_list = lax.dynamic_index_in_dim(matrix, peer_index, 0, keepdims=False)
        rows_here = lax.dynamic_index_in_dim(slot_rows, peer_index, 0, keepdims=False)
        cols_here = lax.dynamic_index_in_dim(slot_cols, peer_index, 0, keepdims=False)
        count_here = lax.dynamic_index_in_dim(slot_counts, peer_index, 0, keepdims=False)
        chosen_entries = jnp.take(panel_rows, cols_here, axis=0)
        block_products = jnp.einsum(
            "wju,wul->wjl", local_block_list, chosen_entries, preferred_element_type=jnp.float32
        )
        selector_mask = (
            (rows_here[:, None] == row_ids[None, :]) & (slot_ids < count_here)[:, None]
        ).astype(jnp.float32)
        reduced_sums = jnp.einsum(
            "pr,pwy->rwy", selector_mask, block_products, precision=lax.Precision.HIGHEST
        )
        return reduced_sums.astype(jnp.bfloat16)

    def store_slab(current, slab, peer_index):
        return lax.dynamic_update_index_in_dim(current, slab, peer_index, 0)

    start_rows = jnp.zeros((panels, shard_rows, pore_count, prolong_width), jnp.bfloat16)
    panel_rows = lax.all_gather(masked, "blk", axis=0, tiled=True)
    shard_total = panel_rows.shape[0] // shard_rows

    def one_shard(shard_step, current):
        present_row_count = lax.dynamic_slice_in_dim(
            panel_rows, shard_step * shard_rows, shard_rows, 0
        )
        return store_slab(current, row_products(shard_step, present_row_count), shard_step)

    collected = lax.fori_loop(0, shard_total, one_shard, start_rows)
    partial_value = jnp.einsum(
        "ixe,pixf->epf", masked, collected, preferred_element_type=jnp.float32
    )
    shares = partial_value.astype(jnp.bfloat16).reshape(3, coarse_width, panels, 3, coarse_width)
    padded = padded_2(shares, (("rows", 0),), 1)
    own_part = padded[2].astype(jnp.float32)
    from_lower = padded[0].astype(jnp.float32)
    from_upper = padded[4].astype(jnp.float32)
    coarse = jnp.pad(own_part, ((0, 0), (0, 0), (1, 1), (0, 0)))
    coarse = coarse + jnp.pad(from_lower, ((0, 0), (0, 0), (0, 2), (0, 0)))
    coarse = coarse + jnp.pad(from_upper, ((0, 0), (0, 0), (2, 0), (0, 0)))
    return coarse[None, None]


def solution(mesh):
    in_specs = (
        P("rows", "blk", None, None, None, None),
        P("rows", "blk", None, None),
        P("rows", "blk", None, None),
        P("rows", "blk", None),
        P("rows", "blk", None, None),
        P("rows", "blk", None),
    )
    out_specs = P("rows", "blk", None, None, None, None)
    return jax.shard_map(
        per_device, mesh=mesh, in_specs=in_specs, out_specs=out_specs, check_vma=False
    )
```

profile of v0, /device:TPU:1, one launch (start us, length us, event | category | flops | bytes accessed | tf_op | source)
XLA Modules:
  0.0 382.4 jit_solution(1796255729361249478)
XLA Ops:
  7.5 2.7 bitcast_multiply_fusion
  11.1 156.9 %all-gather.2.cloned.1.call-done = bf16[256,128,384]{2,1,0:T(8,128)(2,1)} async-done(((bf16[16,128,384]{2,1,0:T(8,128)(2,1)}), bf16[256,128,384]{2,1,0:T(8,128)(2,1)}) %all-gather.2.cloned.1.call-update) | async-done | bytes 25165840 | tf_op jit(solution)/shard_map/all_gather | solution.py:63
  167.9 153.1 %while.14 = (s32[]{:T(128)}, bf16[16,16,128,384]{2,3,1,0:T(8,128)(2,1)}, s32[16,8]{1,0:T(8,128)S(1)}, s32[16]{0:T(128)S(1)}, bf16[16,8,128,128]{3,2,1,0:T(8,128)...) while((s32[]{:T(128)}, ...), condition=%wide.region_1.2_spmd.clone, body=%wide.region_0.1_spmd.clone.sunk | while | flops 177341792 | bytes 16782812 | solution.py:72
  167.9 1.6 constant_dynamic-slice_fusion.4
  172.9 2.2 fusion.45
  177.5 1.6 constant_dynamic-slice_fusion.4
  182.5 2.2 fusion.45
  187.1 1.6 constant_dynamic-slice_fusion.4
  192.0 2.2 fusion.45
  201.6 2.2 fusion.45
  206.3 1.6 constant_dynamic-slice_fusion.4
  211.2 2.2 fusion.45
  220.7 2.2 fusion.45
  230.3 2.2 fusion.45
  239.9 2.2 fusion.45
  249.5 2.2 fusion.45
  259.0 2.2 fusion.45
  268.5 2.2 fusion.45
  278.2 2.2 fusion.45
  287.8 2.2 fusion.45
  297.3 2.2 fusion.45
  306.9 2.2 fusion.45
  316.4 2.2 fusion.45
  321.0 17.0 %bitcast_convert_fusion = bf16[384,16,384]{0,2,1:T(8,128)(2,1)S(1)} fusion(bf16[16,16,128,384]{2,3,1,0:T(8,128)(2,1)} %get-tuple-element.159, bf16[16,128,384]{2,1,0:T(8,128)(2,1)} %bitcast_multiply_fusion), kind=kOutput, calls=%fused_computation.30 | convolution fusion | flops 9666035712 | bytes 31457280 | tf_op jit(solution)/shard_map/ixe,pixf->epf/dot_general | solution.py:73
  338.1 2.5 fusion.28
  340.6 2.8 copy.27
  343.4 3.6 collective-permute-start
  347.0 1.7 copy.28
  348.7 1.9 collective-permute-start.1
  351.8 12.9 %collective-permute-done = bf16[1,128,16,3,128]{4,2,3,1,0:T(8,128)(2,1)} collective-permute-done((bf16[1,128,16,3,128]{4,2,3,1,0:T(8,128)(2,1)}, bf16[1,128,16,3,128]{4,2,3,1,0:T(8,128)(2,1)}, u32[]{:S(2)}, u32[]{:S(2)}) %collective-permute-start) | collective-permute-done | bytes 1572896 | tf_op jit(solution)/shard_map/ppermute | solution.py:14
  364.7 6.1 %collective-permute-done.1 = bf16[1,128,16,3,128]{4,2,3,1,0:T(8,128)(2,1)} collective-permute-done((bf16[1,128,16,3,128]{4,2,3,1,0:T(8,128)(2,1)}, bf16[1,128,16,3,128]{4,2,3,1,0:T(8,128)(2,1)}, u32[]{:S(2)}, u32[]{:S(2)}) %collective-permute-start.1) | collective-permute-done | bytes 1572896 | tf_op jit(solution)/shard_map/ppermute | solution.py:15
  370.8 4.8 %add_bitcast_fusion = f32[1,1,128,16,5,128]{5,3,4,2,1,0:T(8,128)} fusion(bf16[128,16,3,128]{3,1,2,0:T(8,128)(2,1)} %bitcast.12, bf16[128,16,3,128]{3,1,2,0:T(8,128)(2,1)} %bitcast.10, bf16[128,16,3,128]{3,1,2,0:T(8,128)(2,1)S(1)} %copy.26), kind=kLoop, calls=%fused_computation.31 | loop fusion | flops 6553600 | bytes 9961472 | tf_op jit(solution)/shard_map/broadcast_in_dim | solution.py:84
  (190 shorter events, 113.7 us)
Async XLA Ops:
  6.5 161.4 %all-gather.2.cloned.1.call-start = ((), (), s32[]{:S(2)}) async-start(), calls=%async_computation | async-start | bytes 26738688 | tf_op jit(solution)/shard_map/all_gather | solution.py:63
  10.2 0.7 copy-start
  10.2 0.8 copy-start.1
  10.2 157.7 %copy-start.2 = (s32[1,1,16]{2,1,0:T(1,128)S(1)}, s32[1,1,16]{2,1,0:T(1,128)}, u32[]{:S(2)}) copy-start(s32[1,1,16]{2,1,0:T(1,128)} %param.11) | copy-start | bytes 196
  343.4 21.3 %collective-permute-start = (bf16[1,128,16,3,128]{4,2,3,1,0:T(8,128)(2,1)}, bf16[1,128,16,3,128]{4,2,3,1,0:T(8,128)(2,1)}, u32[]{:S(2)}, u32[]{:S(2)}) collective-permute-start(bf16[1,128,16,3,128]{4,2,3,1,0:T(8,128)(2,1)} %copy.27), channel_id=1, source_target_pairs={{0,1},{1,2},{2,3},{3,4},{4,5},{5,6},{6,7},{8,9},{9,10},{10,11},{11... | collective-permute-start | bytes 4718600 | tf_op jit(solution)/shard_map/ppermute | solution.py:14
  348.7 22.0 %collective-permute-start.1 = (bf16[1,128,16,3,128]{4,2,3,1,0:T(8,128)(2,1)}, bf16[1,128,16,3,128]{4,2,3,1,0:T(8,128)(2,1)}, u32[]{:S(2)}, u32[]{:S(2)}) collective-permute-start(bf16[1,128,16,3,128]{4,2,3,1,0:T(8,128)(2,1)} %copy.28), channel_id=1, source_target_pairs={{1,0},{2,1},{3,2},{4,3},{5,4},{6,5},{7,6},{9,8},{10,9},{11,10},{12... | collective-permute-start | bytes 4718600 | tf_op jit(solution)/shard_map/ppermute | solution.py:15
Sparse Core Ops, SparseCore 0:
  10.4 157.5 all-gather.1
where the time goes:
time: 384 us; the launch traced here: 382 us
  waiting for transfers between devices  176 us (46%)
  local copies, waits for them, and re-layouts  94.6 us (25%)
  matrix products  74.1 us (19%)
  other arithmetic  17.7 us (5%)
  between operations  13.5 us (4%)
  starting transfers between devices  5.55 us (1%)
    all_gather x1, waiting for transfers between devices, per_device(): panel_rows = lax.all_gather(masked, 'blk', axis=0, tiled=True)  157 us
    dynamic_update_slice x32, local copies, waits for them, and re-layouts, store_slab(): return lax.dynamic_update_index_in_dim(current, slab, peer_index, 0)  39.3 us
    dot_general x16, matrix products, row_products(): jnp.einsum('pr,pwy->rwy', selector_mask, block_products, precision=lax.Pr...  34.8 us
    dynamic_slice x16, local copies, waits for them, and re-layouts, one_shard(): lax.dynamic_slice_in_dim(panel_rows, shard_step * shard_rows, shard_rows, 0)  25.5 us
    dot_general x16, matrix products, row_products(): jnp.einsum('wju,wul->wjl', local_block_list, chosen_entries, preferred_el...  22.3 us
    dot_general x1, matrix products, per_device(): jnp.einsum('ixe,pixf->epf', masked, collected, preferred_element_type=jnp...  17 us
    ppermute x1, waiting for transfers between devices, padded_2(): before = lax.ppermute(last, axis, up)  12.9 us
    gather x16, local copies, waits for them, and re-layouts, row_products(): chosen_entries = jnp.take(panel_rows, cols_here, axis=0)  11.5 us
  transfers between devices with their start and end apart: 3, of which 3 were waited for; matrix products, arithmetic and copies ran while one was open for 1% of the time, Pallas kernels for 0%

commit v1 on v0

v1 whole, which is shorter than its diff:
```python
import jax
import jax.numpy as jnp
from jax import lax
from jax.experimental import pallas as pl
from jax.experimental.pallas import tpu as pltpu
from jax.sharding import PartitionSpec as P

MESH = pl.DeviceIdType.MESH
BF16 = jnp.bfloat16
F32 = jnp.float32
SIDE = 4
ROWS = 16
CAP = 8
PORES = 128
HALF = 64
WIDTH = 384
GROUPS = 8
PANELS = 16
T_ROWS, T_COUNT, T_MASK, T_ALL = 8, 16, 17, 24


def panel_order(i):
    late = i // 9
    a, b = i // 3, i % 3
    near_z, near_y = a + a // 2, b + b // 2
    k = i + 9 - 18 * late
    s = k // 2
    s = s + s // 2 - 2 * (i // 15)
    odd = k % 2
    far_z = (1 - odd) * s + 2 * odd
    far_y = (1 - odd) * 2 + odd * s
    return near_z * (1 - late) + far_z * late, near_y * (1 - late) + far_y * late


def kernel(
    fine, table, prolong, out,
    stage, amat, vt, yg0, yg1, yg2, yg3, zg0, zg1, zg2, zg3,
    right, pack, relay, tabs, tabs_s, near_s, own, give, got, lt, mid,
    load_sem, tab_send, tab_recv, tab_sem, ring_send, ring_recv, pack_send, relay_send, relay_recv, right_recv,
    give_send, got_recv,
):
    blk, g = lax.axis_index("blk"), lax.axis_index("rows")
    z, y = blk // SIDE, blk % SIDE

    def at(dz, dy):
        return ((z + dz) % SIDE) * SIDE + (y + dy) % SIDE

    def along(axis, d):
        return (at(0, d), g) if axis == 0 else (at(d, 0), g)

    below, above = (blk, (g + GROUPS - 1) % GROUPS), (blk, (g + 1) % GROUPS)

    load_v = pltpu.make_async_copy(prolong, stage, load_sem.at[0])
    load_v.start()
    load_a = pltpu.make_async_copy(fine, amat, load_sem.at[1])
    load_a.start()
    load_t = pltpu.make_async_copy(table, tabs_s, load_sem.at[2])
    load_t.start()

    barrier = pltpu.get_barrier_semaphore()
    friends = [along(axis, d) for axis in range(2) for d in (1, 2, 3)] + [below, above]
    for friend in friends:
        pl.semaphore_signal(barrier, inc=1, device_id=friend, device_id_type=MESH)
    pl.semaphore_wait(barrier, len(friends))

    def remote(src, dst, send, recv, device):
        return pltpu.make_async_remote_copy(
            src_ref=src, dst_ref=dst, send_sem=send, recv_sem=recv, device_id=device, device_id_type=MESH
        )

    sent = []

    def send(*args):
        copy = remote(*args)
        copy.start()
        sent.append(copy)
        return copy

    for axis in range(2):
        for d in (1, 2, 3):
            there = axis * 3 + (SIDE - d) - 1
            here = axis * 3 + d - 1
            copy = remote(
                table.at[pl.ds(0, 8)], tabs.at[there], tab_send.at[here], tab_recv.at[there], along(axis, d)
            )
            copy.start()
            sent.append(copy)

    load_t.wait()
    load_v.wait()

    def mask_row(j, carry):
        blocks = []
        for e in range(3):
            inside = jnp.logical_and(g + e - 1 >= 0, g + e - 1 < GROUPS)
            keep = jnp.logical_and(tabs_s[T_MASK + e, j] == 1, inside)
            keep = jnp.full((PORES, PORES), jnp.where(keep, 1.0, 0.0), F32).astype(BF16)
            blocks.append(stage[j, :, pl.ds(e * PORES, PORES)] * keep)
        row = jnp.concatenate(blocks, axis=1)
        yg0[j] = row[:HALF]
        zg0[j] = row[HALF:]
        return carry

    lax.fori_loop(0, ROWS, mask_row, 0)

    rings = ((yg0, yg1, yg2, yg3), (zg0, zg1, zg2, zg3))
    low, high = pl.ds(0, 8), pl.ds(8, 8)

    def ring_copy(axis, kind):
        r = rings[axis]
        up, down = along(axis, 1), along(axis, 3)
        src, dst, device = {
            0: (r[0].at[low], r[3].at[low], up),
            1: (r[0].at[high], r[1].at[high], down),
            2: (r[0].at[high], r[3].at[high], up),
            3: (r[0].at[low], r[1].at[low], down),
            4: (r[3].at[low], r[2].at[low], up),
            5: (r[1].at[high], r[2].at[high], down),
        }[kind]
        return remote(src, dst, ring_send.at[axis, kind], ring_recv.at[axis, kind], device)

    ring = {(axis, kind): ring_copy(axis, kind) for axis in range(2) for kind in range(6)}
    for kind in range(4):
        for axis in range(2):
            ring[axis, kind].start()

    def turn(j, carry):
        row = jnp.concatenate([yg0[j], zg0[j]], axis=0)
        vt[j] = row.T
        return carry

    lax.fori_loop(0, ROWS, turn, 0)

    for axis in range(2):
        for d in (1, 2, 3):
            slot = axis * 3 + d - 1
            remote(
                table.at[pl.ds(0, 8)], tabs.at[slot], tab_send.at[slot], tab_recv.at[slot], along(axis, d)
            ).wait_recv()
    load_c = pltpu.make_async_copy(tabs, near_s, tab_sem)
    load_c.start()
    load_c.wait()

    def fill(dst, axis, d, who, panel):
        src = rings[axis][d]

        def one(t, carry):
            column = tabs_s[t, panel] if who is None else near_s[who, t, panel]
            dst[t] = src[column]
            return carry

        lax.fori_loop(0, CAP, one, 0)

    def place(axis, d, far):
        return (axis, far, d) if axis == 0 else (axis, d, far)

    def panel_of(axis, d):
        return at(0, d) if axis == 0 else at(d, 0)

    def post(axis, d, t):
        other = 1 - axis
        who = other * 3 + t - 1
        slot = pack.at[axis, t - 1, d]
        fill(slot, axis, d, who, panel_of(axis, d))
        send_sem = pack_send.at[axis, t - 1, d]
        if t == 2:
            way = 0 if d in (0, 1) else 1
            n = 0 if d in (0, 3) else 1
            send(slot, relay.at[axis, way, n], send_sem, relay_recv.at[axis, way, n], along(other, 1 if way == 0 else 3))
        else:
            where = place(axis, d, SIDE - t)
            send(slot, right.at[where], send_sem, right_recv.at[where], along(other, t))

    def keep(axis, d):
        fill(right.at[place(axis, d, 0)], axis, d, None, panel_of(axis, d))

    def post_all(d):
        for t in (2, 1, 3):
            for axis in range(2):
                post(axis, d, t)

    for axis in range(2):
        keep(axis, 0)
    for axis in range(2):
        post(axis, 0, 2)
    for axis in range(2):
        post(axis, 0, 1)
        post(axis, 0, 3)
    for kind in (0, 1):
        for axis in range(2):
            ring[axis, kind].wait_recv()
            ring[axis, kind + 4].start()
    for kind in (2, 3):
        for axis in range(2):
            ring[axis, kind].wait_recv()
    post_all(1)
    post_all(3)

    def forward(axis, way, n):
        other = 1 - axis
        d = ((0, 1), (3, 2))[way][n]
        where = place(axis, d, 2)
        remote(
            pack.at[axis, 1, d], relay.at[axis, way, n], pack_send.at[axis, 1, d], relay_recv.at[axis, way, n],
            along(other, 1 if way == 0 else 3),
        ).wait_recv()
        send(
            relay.at[axis, way, n], right.at[where], relay_send.at[axis, way, n], right_recv.at[where],
            along(other, 1 if way == 0 else 3),
        )

    for kind in (4, 5):
        for axis in range(2):
            ring[axis, kind].wait_recv()
    post_all(2)
    for n in range(2):
        for axis in range(2):
            for way in range(2):
                forward(axis, way, n)
    for axis in range(2):
        for d in (1, 2, 3):
            keep(axis, d)

    load_a.wait()

    def gives(slot):
        return (
            remote(give.at[0, slot], got.at[0, slot], give_send.at[0, slot], got_recv.at[0, slot], below),
            remote(give.at[1, slot], got.at[1, slot], give_send.at[1, slot], got_recv.at[1, slot], above),
        )

    def product(i):
        dz, dy = panel_order(i)
        slot = dz * SIDE + dy
        panel = at(dz, dy)

        def arrived(axis):
            where = (axis, dz, dy)
            remote(
                right.at[where], right.at[where], pack_send.at[0, 0, 0], right_recv.at[where], along(axis, 1)
            ).wait_recv()

        @pl.when(dz > 0)
        def _():
            arrived(0)

        @pl.when(dy > 0)
        def _():
            arrived(1)

        for t in range(CAP):
            span = pl.ds(t * PORES, PORES)
            entry = jnp.concatenate([right[0, dz, dy, t], right[1, dz, dy, t]], axis=0)
            mid[span, :] = jnp.dot(amat[panel, t], entry, preferred_element_type=F32).astype(BF16)
            live = t < tabs_s[T_COUNT, panel]
            live = jnp.full((WIDTH, PORES), jnp.where(live, 1.0, 0.0), F32).astype(BF16)
            lt[:, span] = vt[tabs_s[T_ROWS + t, panel]] * live
        for e, target in ((0, give.at[0, slot]), (2, give.at[1, slot]), (1, own.at[slot])):
            target[...] = jnp.dot(
                lt[pl.ds(e * PORES, PORES), :], mid[...], preferred_element_type=F32
            ).astype(BF16)
        for copy in gives(slot):
            copy.start()

    def finish(i):
        dz, dy = panel_order(i)
        slot = dz * SIDE + dy
        panel = at(dz, dy)
        for copy in gives(slot):
            copy.wait()

        def block(ref, f):
            return ref[:, pl.ds(f * PORES, PORES)].astype(F32)

        for d in range(5):
            value = None
            for ref, f in ((own.at[slot], d - 1), (got.at[1, slot], d), (got.at[0, slot], d - 2)):
                if 0 <= f < 3:
                    term = block(ref, f)
                    value = term if value is None else value + term
            out[pl.ds(d * PANELS + panel, PORES, stride=5 * PANELS), :] = value

    def step(i, carry):
        product(i)

        @pl.when(i >= 2)
        def _():
            finish(i - 2)

        return carry

    lax.fori_loop(0, PANELS, step, 0)
    lax.fori_loop(PANELS - 2, PANELS, lambda i, carry: (finish(i), carry)[1], 0)

    for copy in sent:
        copy.wait_send()
    for copy in ring.values():
        copy.wait_send()


def per_device(fine_blocks, block_rows, block_cols, block_counts, prolong_blocks, prolong_mask):
    table = jnp.concatenate(
        [block_cols[0, 0].T, block_rows[0, 0].T, block_counts[0, 0][None], prolong_mask[0].T], axis=0
    )
    table = jnp.pad(table, ((0, T_ALL - table.shape[0]), (0, PORES - table.shape[1])))
    any_spec = pl.BlockSpec(memory_space=pl.ANY)
    vmem_spec = pl.BlockSpec(memory_space=pltpu.VMEM)
    half_rows = (ROWS, HALF, WIDTH)
    chunk = (CAP, HALF, WIDTH)
    dma = pltpu.SemaphoreType.DMA
    result = pl.pallas_call(
        kernel,
        out_shape=jax.ShapeDtypeStruct((PORES * 5 * PANELS, PORES), F32),
        in_specs=[any_spec, vmem_spec, any_spec],
        out_specs=vmem_spec,
        scratch_shapes=[
            pltpu.VMEM((ROWS, PORES, WIDTH), BF16),
            pltpu.VMEM((PANELS, CAP, PORES, PORES), BF16),
            pltpu.VMEM((ROWS, WIDTH, PORES), BF16),
            *[pltpu.VMEM(half_rows, BF16) for _ in range(8)],
            pltpu.VMEM((2, SIDE, SIDE) + chunk, BF16),
            pltpu.VMEM((2, 3, SIDE) + chunk, BF16),
            pltpu.VMEM((2, 2, 2) + chunk, BF16),
            pltpu.VMEM((6, CAP, PORES), jnp.int32),
            pltpu.SMEM((T_ALL, PORES), jnp.int32),
            pltpu.SMEM((6, CAP, PORES), jnp.int32),
            pltpu.VMEM((PANELS, PORES, WIDTH), BF16),
            pltpu.VMEM((2, PANELS, PORES, WIDTH), BF16),
            pltpu.VMEM((2, PANELS, PORES, WIDTH), BF16),
            pltpu.VMEM((WIDTH, CAP * PORES), BF16),
            pltpu.VMEM((CAP * PORES, WIDTH), BF16),
            dma((3,)),
            dma((6,)),
            dma((6,)),
            dma,
            dma((2, 6)),
            dma((2, 6)),
            dma((2, 3, SIDE)),
            dma((2, 2, 2)),
            dma((2, 2, 2)),
            dma((2, SIDE, SIDE)),
            dma((2, PANELS)),
            dma((2, PANELS)),
        ],
        compiler_params=pltpu.CompilerParams(
            collective_id=0, has_side_effects=True, vmem_limit_bytes=60 * 2**20
        ),
        cost_estimate=pl.CostEstimate(flops=6_500_000_000, bytes_accessed=12_000_000, transcendentals=0),
    )(fine_blocks[0, 0], table, prolong_blocks[0])
    coarse = result.reshape(PORES, 5, PANELS, PORES).transpose(0, 2, 1, 3)
    return coarse[None, None]


def solution(mesh):
    in_specs = (
        P("rows", "blk", None, None, None, None),
        P("rows", "blk", None, None),
        P("rows", "blk", None, None),
        P("rows", "blk", None),
        P("rows", "blk", None, None),
        P("rows", "blk", None),
    )
    out_specs = P("rows", "blk", None, None, None, None)
    return jax.shard_map(
        per_device, mesh=mesh, in_specs=in_specs, out_specs=out_specs, check_vma=False
    )
```

time: 384 us -> 124 us (0.32)
  waiting for transfers between devices: 176 us -> 0 us
  Pallas kernels: 0 us -> 116 us
  local copies, waits for them, and re-layouts: 94.6 us -> 6.47 us
  matrix products: 74.1 us -> 0 us
  other arithmetic: 17.7 us -> 0.73 us
  between operations: 13.5 us -> 0.01 us
  starting transfers between devices: 5.55 us -> 0 us
    all_gather x1 -> x0, waiting for transfers between devices: 157 us -> none  [per_device(): panel_rows = lax.all_gather(masked, 'blk', axis=0, tiled=True)]
    pallas_call x0 -> x1, Pallas kernels: none -> 116 us  [per_device(): pl.pallas_call(kernel, out_shape=jax.ShapeDtypeStruct((PORES * 5 * PANELS...]
    dot_general x33 -> x0, matrix products: 74.1 us -> none  [the longest x16 34.8 us: row_products(): jnp.einsum('pr,pwy->rwy', selector_mask, block_products, precision=lax.Pr...]
    dynamic_update_slice x32 -> x0, local copies, waits for them, and re-layouts: 39.3 us -> none  [store_slab(): return lax.dynamic_update_index_in_dim(current, slab, peer_index, 0)]
    dynamic_slice x32 -> x0, local copies, waits for them, and re-layouts: 34.5 us -> none  [the longest x16 25.5 us: one_shard(): lax.dynamic_slice_in_dim(panel_rows, shard_step * shard_rows, shard_rows, 0)]
    ppermute x2 -> x0, waiting for transfers between devices: 19 us -> none  [the longest x1 12.9 us: padded_2(): before = lax.ppermute(last, axis, up)]
    gather x16 -> x0, local copies, waits for them, and re-layouts: 11.5 us -> none  [row_products(): chosen_entries = jnp.take(panel_rows, cols_here, axis=0)]
    lt x17 -> x0, other arithmetic: 8.84 us -> none  [the longest x16 8.83 us: row_products(): slot_ids < count_here]
  transfers between devices with their start and end apart: 3 -> 0, of which waited for: 3 -> 0; matrix products, arithmetic and copies ran while one was open for 1% -> 0% of each run, Pallas kernels for 0% -> 0%
where the time goes in v1:
time: 124 us; the launch traced here: 123 us
  Pallas kernels  116 us (94%)
  local copies, waits for them, and re-layouts  6.47 us (5%)
    pallas_call x1, Pallas kernels, per_device(): pl.pallas_call(kernel, out_shape=jax.ShapeDtypeStruct((PORES * 5 * PANELS...  116 us
    unnamed x2, local copies, waits for them, and re-layouts  5.87 us

profile of v1, /device:TPU:1, one launch (start us, length us, event | category | flops | bytes accessed | tf_op | source)
XLA Modules:
  0.0 123.1 jit_solution(3373055695095349668)
XLA Ops:
  0.0 0.7 copy.9
  0.7 0.7 pad_add_fusion
  1.4 0.6 pad.4.table
  2.0 115.9 %shard_map.64 = f32[10240,128]{1,0:T(8,128)} custom-call(bf16[16,8,128,128]{3,2,1,0:T(8,128)(2,1)} %bitcast.24, s32[24,128]{1,0:T(8,128)} %pad.4.table, bf16[16,128,384]{2,1,0:T(8,128)(2,1)} %bitcast.25), custom_call_target="tpu_custom_call" | custom-call | flops 6499999744 | bytes 12000000 | tf_op jit(solution)/shard_map/pallas_call | solution.py:311
  117.9 5.2 %copy.11 = f32[1,1,128,16,5,128]{5,3,4,2,1,0:T(8,128)} copy(f32[1,1,128,16,5,128]{5,3,4,2,1,0:T(8,128)} %bitcast.19) | data formatting | bytes 10485760

commit v2 on v1

v2 whole, which is shorter than its diff:
```python
import jax
import jax.numpy as jnp
from jax import lax
from jax.experimental import pallas as pl
from jax.experimental.pallas import tpu as pltpu
from jax.sharding import PartitionSpec as P

MESH = pl.DeviceIdType.MESH
BF16 = jnp.bfloat16
F32 = jnp.float32
SIDE = 4
ROWS = 16
CAP = 8
PORES = 128
HALF = 64
WIDTH = 384
GROUPS = 8
PANELS = 16
EARLY = 5
ORDER = (
    (0, 0), (0, 1), (1, 0), (0, 3), (3, 0),
    (0, 2), (2, 0), (1, 1), (1, 3), (3, 1), (3, 3), (2, 1), (1, 2), (2, 3), (3, 2), (2, 2),
)


def pick(values, i):
    n = len(values)
    total = values[0]
    for k in range(1, n):
        if values[k] != values[k - 1]:
            total = total + (values[k] - values[k - 1]) * ((i + n - k) // n)
    return total


def kernel(
    fine, prolong, cols_h, rows_h, counts_h, mask_h, out,
    stage, amat, vt, yg0, yg1, yg2, yg3, zg0, zg1, zg2, zg3,
    right, pack, tabs, cols, rows, counts, mask, near_s, own, give, got, lt, mid,
    load_sem, tab_send, tab_recv, tab_sem, ring_send, ring_recv, pack_send, right_recv, give_send, got_recv,
):
    blk, g = lax.axis_index("blk"), lax.axis_index("rows")
    z, y = blk // SIDE, blk % SIDE

    def at(dz, dy):
        return ((z + dz) % SIDE) * SIDE + (y + dy) % SIDE

    def along(axis, d):
        return (at(0, d), g) if axis == 0 else (at(d, 0), g)

    below, above = (blk, (g + GROUPS - 1) % GROUPS), (blk, (g + 1) % GROUPS)

    barrier = pltpu.get_barrier_semaphore()
    friends = [along(axis, d) for axis in range(2) for d in (1, 2, 3)] + [below, above]
    for friend in friends:
        pl.semaphore_signal(barrier, inc=1, device_id=friend, device_id_type=MESH)

    loads = [
        pltpu.make_async_copy(src, dst, load_sem.at[n])
        for n, (src, dst) in enumerate(
            ((prolong, stage), (mask_h, mask), (cols_h, cols), (rows_h, rows), (counts_h, counts), (fine, amat))
        )
    ]
    for load in loads:
        load.start()

    def remote(src, dst, send, recv, device):
        return pltpu.make_async_remote_copy(
            src_ref=src, dst_ref=dst, send_sem=send, recv_sem=recv, device_id=device, device_id_type=MESH
        )

    sent = []

    def send(*args):
        copy = remote(*args)
        copy.start()
        sent.append(copy)

    for load in loads[:2]:
        load.wait()

    def mask_row(j, carry):
        blocks = []
        for e in range(3):
            inside = jnp.logical_and(g + e - 1 >= 0, g + e - 1 < GROUPS)
            keep = jnp.logical_and(mask[e, 0, j] == 1, inside)
            keep = jnp.full((PORES, PORES), jnp.where(keep, 1.0, 0.0), F32).astype(BF16)
            blocks.append(stage[j, :, pl.ds(e * PORES, PORES)] * keep)
        row = jnp.concatenate(blocks, axis=1)
        yg0[j] = row[:HALF]
        zg0[j] = row[HALF:]
        return carry

    lax.fori_loop(0, ROWS, mask_row, 0)
    pl.semaphore_wait(barrier, len(friends))

    rings = ((yg0, yg1, yg2, yg3), (zg0, zg1, zg2, zg3))
    low, high = pl.ds(0, 8), pl.ds(8, 8)

    def ring_copy(axis, kind):
        r = rings[axis]
        up, down = along(axis, 1), along(axis, 3)
        src, dst, device = {
            0: (r[0].at[low], r[3].at[low], up),
            1: (r[0].at[high], r[1].at[high], down),
            2: (r[0].at[high], r[3].at[high], up),
            3: (r[0].at[low], r[1].at[low], down),
            4: (r[3].at[low], r[2].at[low], up),
            5: (r[1].at[high], r[2].at[high], down),
        }[kind]
        return remote(src, dst, ring_send.at[axis, kind], ring_recv.at[axis, kind], device)

    ring = {(axis, kind): ring_copy(axis, kind) for axis in range(2) for kind in range(6)}

    def tab_copy(axis, d, slot):
        return remote(cols_h, tabs.at[slot], tab_send.at[axis * 3 + d - 1], tab_recv.at[slot], along(axis, d))

    for axis in range(2):
        for d in (1, 2, 3):
            copy = tab_copy(axis, d, axis * 3 + (SIDE - d) - 1)
            copy.start()
            sent.append(copy)
    for kind in range(4):
        for axis in range(2):
            ring[axis, kind].start()

    def turn(j, carry):
        row = jnp.concatenate([yg0[j], zg0[j]], axis=0)
        vt[j] = row.T
        return carry

    for load in loads[2:5]:
        load.wait()
    for axis in range(2):
        for d in (1, 2, 3):
            tab_copy(axis, d, axis * 3 + d - 1).wait_recv()
    load_c = pltpu.make_async_copy(tabs, near_s, tab_sem)
    load_c.start()
    load_c.wait()

    def fill(dst, axis, d, who):
        src = rings[axis][d]
        panel = at(0, d) if axis == 0 else at(d, 0)

        def one(t, carry):
            column = cols[t, panel] if who is None else near_s[who, t, panel]
            dst[t] = src[column]
            return carry

        lax.fori_loop(0, CAP, one, 0)

    def place(axis, d, far):
        return (axis, far, d) if axis == 0 else (axis, d, far)

    def post(axis, d, t):
        other = 1 - axis
        slot = pack.at[axis, t - 1, d]
        fill(slot, axis, d, other * 3 + t - 1)
        where = place(axis, d, SIDE - t)
        send(slot, right.at[where], pack_send.at[axis, t - 1, d], right_recv.at[where], along(other, t))

    def post_all(d):
        for t in (1, 3, 2):
            for axis in range(2):
                post(axis, d, t)

    def keep(axis, d):
        fill(right.at[place(axis, d, 0)], axis, d, None)

    post_all(0)
    for kind in (0, 1):
        for axis in range(2):
            ring[axis, kind].wait_recv()
            ring[axis, kind + 4].start()
    lax.fori_loop(0, ROWS, turn, 0)
    for kind in (2, 3):
        for axis in range(2):
            ring[axis, kind].wait_recv()
    post_all(1)
    post_all(3)
    for d in (0, 1, 3):
        for axis in range(2):
            keep(axis, d)
    loads[5].wait()

    def gives(slot):
        return (
            remote(give.at[0, slot], got.at[0, slot], give_send.at[0, slot], got_recv.at[0, slot], below),
            remote(give.at[1, slot], got.at[1, slot], give_send.at[1, slot], got_recv.at[1, slot], above),
        )

    def offsets(i):
        dz, dy = pick([p[0] for p in ORDER], i), pick([p[1] for p in ORDER], i)
        return dz, dy, dz * SIDE + dy, at(dz, dy)

    def product(i):
        dz, dy, slot, panel = offsets(i)

        def arrived(axis):
            where = right.at[axis, dz, dy]
            remote(where, where, pack_send.at[0, 0, 0], right_recv.at[axis, dz, dy], along(axis, 1)).wait_recv()

        @pl.when(dz > 0)
        def _():
            arrived(0)

        @pl.when(dy > 0)
        def _():
            arrived(1)

        for t in range(CAP):
            span = pl.ds(t * PORES, PORES)
            entry = jnp.concatenate([right[0, dz, dy, t], right[1, dz, dy, t]], axis=0)
            mid[span, :] = jnp.dot(amat[panel, t], entry, preferred_element_type=F32).astype(BF16)
            live = t < counts[0, panel]
            live = jnp.full((WIDTH, PORES), jnp.where(live, 1.0, 0.0), F32).astype(BF16)
            lt[:, span] = vt[rows[t, panel]] * live
        below_copy, above_copy = gives(slot)
        for e, target in ((0, give.at[0, slot]), (2, give.at[1, slot]), (1, own.at[slot])):
            target[...] = jnp.dot(
                lt[pl.ds(e * PORES, PORES), :], mid[...], preferred_element_type=F32
            ).astype(BF16)
            if e == 0:
                below_copy.start()
            if e == 2:
                above_copy.start()

    def finish(i):
        dz, dy, slot, panel = offsets(i)
        for copy in gives(slot):
            copy.wait()

        def block(ref, f):
            return ref[:, pl.ds(f * PORES, PORES)].astype(F32)

        for d in range(5):
            value = None
            for ref, f in ((own.at[slot], d - 1), (got.at[1, slot], d), (got.at[0, slot], d - 2)):
                if 0 <= f < 3:
                    term = block(ref, f)
                    value = term if value is None else value + term
            out[pl.ds(d * PANELS + panel, PORES, stride=5 * PANELS), :] = value

    def step(i, carry):
        product(i)

        @pl.when(i >= 2)
        def _():
            finish(i - 2)

        return carry

    lax.fori_loop(0, EARLY, step, 0)
    for kind in (4, 5):
        for axis in range(2):
            ring[axis, kind].wait_recv()
    post_all(2)
    for axis in range(2):
        keep(axis, 2)
    lax.fori_loop(EARLY, PANELS, step, 0)
    lax.fori_loop(PANELS - 2, PANELS, lambda i, carry: (finish(i), carry)[1], 0)

    for copy in sent:
        copy.wait_send()
    for copy in ring.values():
        copy.wait_send()


def per_device(fine_blocks, block_rows, block_cols, block_counts, prolong_blocks, prolong_mask):
    any_spec = pl.BlockSpec(memory_space=pl.ANY)
    half_rows = (ROWS, HALF, WIDTH)
    chunk = (CAP, HALF, WIDTH)
    dma = pltpu.SemaphoreType.DMA
    result = pl.pallas_call(
        kernel,
        out_shape=pltpu.VMEM((PORES * 5 * PANELS, PORES), F32),
        in_specs=[any_spec] * 6,
        out_specs=pl.BlockSpec(memory_space=pltpu.VMEM),
        scratch_shapes=[
            pltpu.VMEM((ROWS, PORES, WIDTH), BF16),
            pltpu.VMEM((PANELS, CAP, PORES, PORES), BF16),
            pltpu.VMEM((ROWS, WIDTH, PORES), BF16),
            *[pltpu.VMEM(half_rows, BF16) for _ in range(8)],
            pltpu.VMEM((2, SIDE, SIDE) + chunk, BF16),
            pltpu.VMEM((2, 3, SIDE) + chunk, BF16),
            pltpu.VMEM((6, CAP, PANELS), jnp.int32),
            pltpu.SMEM((CAP, PANELS), jnp.int32),
            pltpu.SMEM((CAP, PANELS), jnp.int32),
            pltpu.SMEM((1, PANELS), jnp.int32),
            pltpu.SMEM((3, 1, ROWS), jnp.int32),
            pltpu.SMEM((6, CAP, PANELS), jnp.int32),
            pltpu.VMEM((PANELS, PORES, WIDTH), BF16),
            pltpu.VMEM((2, PANELS, PORES, WIDTH), BF16),
            pltpu.VMEM((2, PANELS, PORES, WIDTH), BF16),
            pltpu.VMEM((WIDTH, CAP * PORES), BF16),
            pltpu.VMEM((CAP * PORES, WIDTH), BF16),
            dma((6,)),
            dma((6,)),
            dma((6,)),
            dma,
            dma((2, 6)),
            dma((2, 6)),
            dma((2, 3, SIDE)),
            dma((2, SIDE, SIDE)),
            dma((2, PANELS)),
            dma((2, PANELS)),
        ],
        compiler_params=pltpu.CompilerParams(
            collective_id=0, has_side_effects=True, vmem_limit_bytes=50 * 2**20
        ),
        cost_estimate=pl.CostEstimate(flops=6_500_000_000, bytes_accessed=12_000_000, transcendentals=0),
    )(
        fine_blocks[0, 0],
        prolong_blocks[0],
        block_cols[0, 0].T,
        block_rows[0, 0].T,
        block_counts[0],
        prolong_mask.transpose(2, 0, 1),
    )
    coarse = result.reshape(PORES, 5, PANELS, PORES).transpose(0, 2, 1, 3)
    return coarse[None, None]


def solution(mesh):
    in_specs = (
        P("rows", "blk", None, None, None, None),
        P("rows", "blk", None, None),
        P("rows", "blk", None, None),
        P("rows", "blk", None),
        P("rows", "blk", None, None),
        P("rows", "blk", None),
    )
    out_specs = P("rows", "blk", None, None, None, None)
    return jax.shard_map(
        per_device, mesh=mesh, in_specs=in_specs, out_specs=out_specs, check_vma=False
    )
```

time: 124 us -> 111 us (0.90)
  Pallas kernels: 116 us -> 108 us
  local copies, waits for them, and re-layouts: 6.47 us -> 2.36 us
    pallas_call x1, Pallas kernels: 116 us -> 108 us  [per_device(): pl.pallas_call(kernel, out_shape=pltpu.VMEM((PORES * 5 * PANELS, PORES),...]
    unnamed x2 -> x1, local copies, waits for them, and re-layouts: 5.87 us -> 2.36 us
where the time goes in v2:
time: 111 us
  Pallas kernels  108 us (97%)
  local copies, waits for them, and re-layouts  2.36 us (2%)
    pallas_call x1, Pallas kernels, per_device(): pl.pallas_call(kernel, out_shape=pltpu.VMEM((PORES * 5 * PANELS, PORES),...  108 us
    unnamed x1, local copies, waits for them, and re-layouts  2.36 us

profile of v2, /device:TPU:1, one launch (start us, length us, event | category | flops | bytes accessed | tf_op | source)
XLA Modules:
  0.0 110.7 jit_solution(12445856166405360774)
XLA Ops:
  0.0 108.3 %shard_map.64 = f32[10240,128]{1,0:T(8,128)S(1)} custom-call(bf16[16,8,128,128]{3,2,1,0:T(8,128)(2,1)} %bitcast.16, bf16[16,128,384]{2,1,0:T(8,128)(2,1)} %bitcast.17, s32[8,16]{1,0:T(8,128)} %bitcast.18, s32[8,16]{1,0:T(8,128)} %bitcast.19, s32[1,16]{1,0:T(1,128)} %bitcast.21, s32[3,1,16]{2,1,0:T(1,128)} %bitcast.20), custom_call_target="tpu_custom_call" | custom-call | flops 6499999744 | bytes 12000000 | tf_op jit(solution)/shard_map/pallas_call | solution.py:273
  108.3 2.4 %copy.8 = f32[1,1,128,16,5,128]{5,3,4,2,1,0:T(8,128)} copy(f32[1,1,128,16,5,128]{5,3,4,2,1,0:T(8,128)S(1)} %bitcast.15) | data formatting | bytes 10485760

commit v3 on v2

v3 whole, which is shorter than its diff:
```python
import jax
import jax.numpy as jnp
from jax import lax
from jax.experimental import pallas as pl
from jax.experimental.pallas import tpu as pltpu
from jax.sharding import PartitionSpec as P

MESH = pl.DeviceIdType.MESH
BF16 = jnp.bfloat16
F32 = jnp.float32
SIDE = 4
ROWS = 16
CAP = 8
PORES = 128
WIDTH = 384
GROUPS = 8
PANELS = 16
OFFSETS = 5
T_ROWS, T_COUNT, T_ALL = 8, 16, 24
HELD = ((0, 0), (0, 1), (0, 3), (1, 0), (3, 0), (0, 2), (2, 0))
NEAR, LOCAL = 5, 7
SENT = (
    ((2, 2), (0, 2)), ((2, 1), (0, 1)), ((1, 3), (0, 3)), ((1, 1), (1, 0)), ((3, 3), (3, 0)),
    ((2, 3), (0, 3)), ((1, 2), (1, 0)), ((3, 1), (3, 0)), ((3, 2), (3, 0)),
)


def minus(p, q):
    return (p[0] - q[0]) % SIDE, (p[1] - q[1]) % SIDE


LISTER = tuple(HELD.index(minus((0, 0), h)) for _, h in SENT)
COLUMN = tuple(HELD.index(minus(p, h)) for p, h in SENT)


def pick(values, i):
    n = len(values)
    total = values[0]
    for k in range(1, n):
        if values[k] != values[k - 1]:
            total = total + (values[k] - values[k - 1]) * ((i + n - k) // n)
    return total


def kernel(
    fine, prolong, cols_h, rows_h, counts_h, mask_h, out,
    stage, amat, held, far, turned, tab, tabs, counts, mask, tabs_s,
    listed, own, give, got, result, returned, lt, mid,
    load_sem, tab_send, tab_recv, tab_sem, ring_send, ring_recv, list_send, list_recv, give_send, got_recv,
    result_send, result_recv,
):
    blk, g = lax.axis_index("blk"), lax.axis_index("rows")
    z, y = blk // SIDE, blk % SIDE

    def at(offset):
        dz, dy = offset
        return ((z + dz) % SIDE) * SIDE + (y + dy) % SIDE

    def device(offset):
        return at(offset), g

    below, above = (blk, (g + GROUPS - 1) % GROUPS), (blk, (g + 1) % GROUPS)

    barrier = pltpu.get_barrier_semaphore()
    friends = [device(offset) for offset in HELD[1:6]] + [below, above]
    for friend in friends:
        pl.semaphore_signal(barrier, inc=1, device_id=friend, device_id_type=MESH)

    loads = [
        pltpu.make_async_copy(src, dst, load_sem.at[n])
        for n, (src, dst) in enumerate(
            (
                (prolong, stage),
                (mask_h, mask),
                (cols_h, tab.at[pl.ds(0, CAP)]),
                (rows_h, tab.at[pl.ds(T_ROWS, CAP)]),
                (counts_h, counts),
                (fine, amat),
            )
        )
    ]
    for load in loads:
        load.start()

    def remote(src, dst, send, recv, target):
        return pltpu.make_async_remote_copy(
            src_ref=src, dst_ref=dst, send_sem=send, recv_sem=recv, device_id=target, device_id_type=MESH
        )

    for load in loads[:2]:
        load.wait()

    def mask_row(j, carry):
        for e in range(3):
            inside = jnp.logical_and(g + e - 1 >= 0, g + e - 1 < GROUPS)
            keep = jnp.logical_and(mask[e, 0, j] == 1, inside)
            keep = jnp.full((PORES, PORES), jnp.where(keep, 1.0, 0.0), F32).astype(BF16)
            span = pl.ds(e * PORES, PORES)
            held[0, j, :, span] = stage[j, :, span] * keep
        return carry

    lax.fori_loop(0, ROWS, mask_row, 0)
    for load in loads[2:5]:
        load.wait()
    tab[pl.ds(T_COUNT, CAP), :] = jnp.broadcast_to(counts[...], (CAP, PANELS))
    pl.semaphore_wait(barrier, len(friends))

    def tab_copy(n, target):
        return remote(tab, tabs.at[n], tab_send.at[n], tab_recv.at[n], target)

    for n in range(1, 6):
        tab_copy(n, device(minus((0, 0), HELD[n]))).start()

    low, high = pl.ds(0, 8), pl.ds(8, 8)

    def ring_copy(axis, kind):
        next_at, last_at = 1 + 2 * axis, 2 + 2 * axis
        up, down = device(HELD[next_at]), device(HELD[last_at])
        src, dst, target = {
            0: (held.at[0, low], held.at[last_at, low], up),
            1: (held.at[0, high], held.at[next_at, high], down),
            2: (held.at[0, high], held.at[last_at, high], up),
            3: (held.at[0, low], held.at[next_at, low], down),
            4: (held.at[last_at, low], far.at[axis, low], up),
            5: (held.at[next_at, high], far.at[axis, high], down),
        }[kind]
        return remote(src, dst, ring_send.at[axis, kind], ring_recv.at[axis, kind], target)

    ring = {(axis, kind): ring_copy(axis, kind) for axis in range(2) for kind in range(6)}
    for kind in range(4):
        for axis in range(2):
            ring[axis, kind].start()

    def turn(n):
        def one(j, carry):
            turned[n, j] = held[n, j].T
            return carry

        lax.fori_loop(0, ROWS, one, 0)

    turn(0)
    for n in range(1, 6):
        tab_copy(n, device(HELD[n])).wait_recv()
    copies = [
        pltpu.make_async_copy(tab, tabs_s.at[0], tab_sem.at[0]),
        pltpu.make_async_copy(tabs.at[pl.ds(1, 5)], tabs_s.at[pl.ds(1, 5)], tab_sem.at[1]),
    ]
    for copy in copies:
        copy.start()
    for copy in copies:
        copy.wait()
    loads[5].wait()

    for kind in (0, 1):
        for axis in range(2):
            ring[axis, kind].wait_recv()
            ring[axis, kind + 4].start()

    def list_copy(k):
        panel, worker = SENT[k]
        return remote(amat.at[at(panel)], listed.at[k], list_send.at[k], list_recv.at[k], device(worker))

    for k in range(len(SENT)):
        list_copy(k).start()
    for kind in (2, 3):
        for axis in range(2):
            ring[axis, kind].wait_recv()
    for n in range(1, NEAR):
        turn(n)

    def gives(slot):
        return (
            remote(give.at[0, slot], got.at[0, slot], give_send.at[0, slot], got_recv.at[0, slot], below),
            remote(give.at[1, slot], got.at[1, slot], give_send.at[1, slot], got_recv.at[1, slot], above),
        )

    def product(slot, blocks, lister, column, panel):
        for t in range(CAP):
            span = pl.ds(t * PORES, PORES)
            entry = held[column, tabs_s[lister, t, panel]]
            mid[span, :] = jnp.dot(blocks[t], entry, preferred_element_type=F32).astype(BF16)
            live = t < tabs_s[lister, T_COUNT, panel]
            live = jnp.full((WIDTH, PORES), jnp.where(live, 1.0, 0.0), F32).astype(BF16)
            lt[:, span] = turned[lister, tabs_s[lister, T_ROWS + t, panel]] * live
        below_copy, above_copy = gives(slot)
        for e, target in ((0, give.at[0, slot]), (2, give.at[1, slot]), (1, own.at[slot])):
            target[...] = jnp.dot(
                lt[pl.ds(e * PORES, PORES), :], mid[...], preferred_element_type=F32
            ).astype(BF16)
            if e == 0:
                below_copy.start()
            if e == 2:
                above_copy.start()

    def summed(slot):
        for copy in gives(slot):
            copy.wait()

        def block(ref, f):
            return ref[:, pl.ds(f * PORES, PORES)].astype(F32)

        values = []
        for d in range(OFFSETS):
            value = None
            for ref, f in ((own.at[slot], d - 1), (got.at[1, slot], d), (got.at[0, slot], d - 2)):
                if 0 <= f < 3:
                    term = block(ref, f)
                    value = term if value is None else value + term
            values.append(value)
        return values

    def store(values, panel):
        for d, value in enumerate(values):
            out[pl.ds(d * PANELS + panel, PORES, stride=OFFSETS * PANELS), :] = value

    def held_panel(i):
        return at((pick([p[0] for p in HELD], i), pick([p[1] for p in HELD], i)))

    def local_step(i, carry):
        panel = held_panel(i)
        product(i, amat.at[panel], 0, i, panel)

        @pl.when(i >= 2)
        def _():
            store(summed(i - 2), held_panel(i - 2))

        return carry

    def back(k):
        lister = (pick([HELD[n][0] for n in LISTER], k), pick([HELD[n][1] for n in LISTER], k))
        return remote(result.at[k], returned.at[k], result_send.at[k], result_recv.at[k], device(lister))

    def give_back(k):
        for d, value in enumerate(summed(k + LOCAL)):
            result[k, :, pl.ds(d * PORES, PORES)] = value.astype(BF16)
        back(k).start()

    def sent_step(k, carry):
        lister, column = pick(LISTER, k), pick(COLUMN, k)
        panel = held_panel(column)
        remote(listed.at[k], listed.at[k], list_send.at[k], list_recv.at[k], below).wait_recv()
        product(k + LOCAL, listed.at[k], lister, column, panel)

        @pl.when(k >= 2)
        def _():
            give_back(k - 2)

        return carry

    lax.fori_loop(0, NEAR, local_step, 0)
    for kind in (4, 5):
        for axis in range(2):
            ring[axis, kind].wait_recv()

    def settle(j, carry):
        for axis in range(2):
            held[NEAR + axis, j] = far[axis, j]
        return carry

    lax.fori_loop(0, ROWS, settle, 0)
    turn(NEAR)
    lax.fori_loop(NEAR, LOCAL, local_step, 0)
    for i in range(LOCAL - 2, LOCAL):
        store(summed(i), held_panel(i))
    last = len(SENT)
    lax.fori_loop(0, last, sent_step, 0)
    lax.fori_loop(last - 2, last, lambda k, carry: (give_back(k), carry)[1], 0)

    def arrive(k, carry):
        panel = at((pick([p[0] for p, _ in SENT], k), pick([p[1] for p, _ in SENT], k)))
        back(k).wait_recv()
        store([returned[k, :, pl.ds(d * PORES, PORES)].astype(F32) for d in range(OFFSETS)], panel)
        return carry

    lax.fori_loop(0, last, arrive, 0)

    for n in range(1, 6):
        tab_copy(n, device(minus((0, 0), HELD[n]))).wait_send()
    for copy in ring.values():
        copy.wait_send()
    for k in range(last):
        list_copy(k).wait_send()
        back(k).wait_send()


def per_device(fine_blocks, block_rows, block_cols, block_counts, prolong_blocks, prolong_mask):
    any_spec = pl.BlockSpec(memory_space=pl.ANY)
    dma = pltpu.SemaphoreType.DMA
    sent = len(SENT)
    value = pl.pallas_call(
        kernel,
        out_shape=pltpu.VMEM((PORES * OFFSETS * PANELS, PORES), F32),
        in_specs=[any_spec] * 6,
        out_specs=pl.BlockSpec(memory_space=pltpu.VMEM),
        scratch_shapes=[
            pltpu.VMEM((ROWS, PORES, WIDTH), BF16),
            pltpu.VMEM((PANELS, CAP, PORES, PORES), BF16),
            pltpu.VMEM((LOCAL, ROWS, PORES, WIDTH), BF16),
            pltpu.VMEM((2, ROWS, PORES, WIDTH), BF16),
            pltpu.VMEM((6, ROWS, WIDTH, PORES), BF16),
            pltpu.VMEM((T_ALL, PANELS), jnp.int32),
            pltpu.VMEM((6, T_ALL, PANELS), jnp.int32),
            pltpu.VMEM((1, PANELS), jnp.int32),
            pltpu.SMEM((3, 1, ROWS), jnp.int32),
            pltpu.SMEM((6, T_ALL, PANELS), jnp.int32),
            pltpu.VMEM((sent, CAP, PORES, PORES), BF16),
            pltpu.VMEM((PANELS, PORES, WIDTH), BF16),
            pltpu.VMEM((2, PANELS, PORES, WIDTH), BF16),
            pltpu.VMEM((2, PANELS, PORES, WIDTH), BF16),
            pltpu.VMEM((sent, PORES, OFFSETS * PORES), BF16),
            pltpu.VMEM((sent, PORES, OFFSETS * PORES), BF16),
            pltpu.VMEM((WIDTH, CAP * PORES), BF16),
            pltpu.VMEM((CAP * PORES, WIDTH), BF16),
            dma((6,)),
            dma((6,)),
            dma((6,)),
            dma((2,)),
            dma((2, 6)),
            dma((2, 6)),
            dma((sent,)),
            dma((sent,)),
            dma((2, PANELS)),
            dma((2, PANELS)),
            dma((sent,)),
            dma((sent,)),
        ],
        compiler_params=pltpu.CompilerParams(
            collective_id=0, has_side_effects=True, vmem_limit_bytes=52 * 2**20
        ),
        cost_estimate=pl.CostEstimate(flops=6_500_000_000, bytes_accessed=12_000_000, transcendentals=0),
    )(
        fine_blocks[0, 0],
        prolong_blocks[0],
        block_cols[0, 0].T,
        block_rows[0, 0].T,
        block_counts[0],
        prolong_mask.transpose(2, 0, 1),
    )
    coarse = value.reshape(PORES, OFFSETS, PANELS, PORES).transpose(0, 2, 1, 3)
    return coarse[None, None]


def solution(mesh):
    in_specs = (
        P("rows", "blk", None, None, None, None),
        P("rows", "blk", None, None),
        P("rows", "blk", None, None),
        P("rows", "blk", None),
        P("rows", "blk", None, None),
        P("rows", "blk", None),
    )
    out_specs = P("rows", "blk", None, None, None, None)
    return jax.shard_map(
        per_device, mesh=mesh, in_specs=in_specs, out_specs=out_specs, check_vma=False
    )
```

time: 111 us -> 101 us (0.910); the launches traced: 111 us -> 99.3 us
  Pallas kernels: 108 us -> 96.9 us
    pallas_call x1, Pallas kernels: 108 us -> 96.9 us  [per_device(): pl.pallas_call(kernel, out_shape=pltpu.VMEM((PORES * OFFSETS * PANELS, PO...]
where the time goes in v3:
time: 101 us; the launch traced here: 99.3 us
  Pallas kernels  96.9 us (96%)
  local copies, waits for them, and re-layouts  2.36 us (2%)
    pallas_call x1, Pallas kernels, per_device(): pl.pallas_call(kernel, out_shape=pltpu.VMEM((PORES * OFFSETS * PANELS, PO...  96.9 us
    unnamed x1, local copies, waits for them, and re-layouts  2.36 us

profile of v3, /device:TPU:1, one launch (start us, length us, event | category | flops | bytes accessed | tf_op | source)
XLA Modules:
  0.0 99.3 jit_solution(9152331532392628715)
XLA Ops:
  0.0 96.9 %shard_map.64 = f32[10240,128]{1,0:T(8,128)S(1)} custom-call(bf16[16,8,128,128]{3,2,1,0:T(8,128)(2,1)} %bitcast.16, bf16[16,128,384]{2,1,0:T(8,128)(2,1)} %bitcast.17, s32[8,16]{1,0:T(8,128)} %bitcast.18, s32[8,16]{1,0:T(8,128)} %bitcast.19, s32[1,16]{1,0:T(1,128)} %bitcast.21, s32[3,1,16]{2,1,0:T(1,128)} %bitcast.20), custom_call_target="tpu_custom_call" | custom-call | flops 6499999744 | bytes 12000000 | tf_op jit(solution)/shard_map/pallas_call | solution.py:290
  97.0 2.4 %copy.8 = f32[1,1,128,16,5,128]{5,3,4,2,1,0:T(8,128)} copy(f32[1,1,128,16,5,128]{5,3,4,2,1,0:T(8,128)S(1)} %bitcast.15) | data formatting | bytes 10485760

commit v4 on v3

--- a/solution.py
+++ b/solution.py
@@ -20,9 +20,11 @@
 HELD = ((0, 0), (0, 1), (0, 3), (1, 0), (3, 0), (0, 2), (2, 0))
 NEAR, LOCAL = 5, 7
 SENT = (
-    ((2, 2), (0, 2)), ((2, 1), (0, 1)), ((1, 3), (0, 3)), ((1, 1), (1, 0)), ((3, 3), (3, 0)),
-    ((2, 3), (0, 3)), ((1, 2), (1, 0)), ((3, 1), (3, 0)), ((3, 2), (3, 0)),
+    ((2, 2), (0, 2)),
+    ((2, 1), (0, 1)), ((2, 3), (0, 3)), ((1, 2), (1, 0)), ((3, 2), (3, 0)),
+    ((3, 1), (0, 1)), ((1, 3), (0, 3)), ((1, 1), (1, 0)), ((3, 3), (3, 0)),
 )
+ACROSS = 0
 
 
 def minus(p, q):
@@ -31,26 +33,33 @@
 
 LISTER = tuple(HELD.index(minus((0, 0), h)) for _, h in SENT)
 COLUMN = tuple(HELD.index(minus(p, h)) for p, h in SENT)
+IS_ACROSS = tuple(int(k == ACROSS) for k in range(len(SENT)))
+STEPS = ((0, 1, 2, 3, 4), (7, 5, 6, 8, 9, 10, 11), (12, 13, 14, 15))
+ORDER = sum(STEPS, ())
+STARTS = tuple(sum(len(s) for s in STEPS[:n]) for n in range(len(STEPS) + 1))
 
 
 def pick(values, i):
-    n = len(values)
+    if isinstance(i, int):
+        return values[i]
     total = values[0]
-    for k in range(1, n):
+    for k in range(1, len(values)):
         if values[k] != values[k - 1]:
-            total = total + (values[k] - values[k - 1]) * ((i + n - k) // n)
+            total = total + (values[k] - values[k - 1]) * (i >= k).astype(jnp.int32)
     return total
 
 
 def kernel(
     fine, prolong, cols_h, rows_h, counts_h, mask_h, out,
-    stage, amat, held, far, turned, tab, tabs, counts, mask, tabs_s,
-    listed, own, give, got, result, returned, lt, mid,
+    stage, blocks, held, far_y, far_z, turned, tab, tabs, counts, mask, tabs_s,
+    own, give, got, result, returned, lt,
     load_sem, tab_send, tab_recv, tab_sem, ring_send, ring_recv, list_send, list_recv, give_send, got_recv,
     result_send, result_recv,
 ):
     blk, g = lax.axis_index("blk"), lax.axis_index("rows")
     z, y = blk // SIDE, blk % SIDE
+    odd = (z + y) % 2
+    across = (2 * odd, 2 * (1 - odd))
 
     def at(offset):
         dz, dy = offset
@@ -62,7 +71,7 @@
     below, above = (blk, (g + GROUPS - 1) % GROUPS), (blk, (g + 1) % GROUPS)
 
     barrier = pltpu.get_barrier_semaphore()
-    friends = [device(offset) for offset in HELD[1:6]] + [below, above]
+    friends = [device(offset) for offset in HELD[1:NEAR] + (across,)] + [below, above]
     for friend in friends:
         pl.semaphore_signal(barrier, inc=1, device_id=friend, device_id_type=MESH)
 
@@ -75,7 +84,7 @@
                 (cols_h, tab.at[pl.ds(0, CAP)]),
                 (rows_h, tab.at[pl.ds(T_ROWS, CAP)]),
                 (counts_h, counts),
-                (fine, amat),
+                (fine, blocks.at[pl.ds(0, PANELS)]),
             )
         )
     ]
@@ -108,21 +117,23 @@
     def tab_copy(n, target):
         return remote(tab, tabs.at[n], tab_send.at[n], tab_recv.at[n], target)
 
+    tab_targets = [minus((0, 0), HELD[n]) for n in range(1, NEAR)] + [across]
     for n in range(1, 6):
-        tab_copy(n, device(minus((0, 0), HELD[n]))).start()
+        tab_copy(n, device(tab_targets[n - 1])).start()
 
     low, high = pl.ds(0, 8), pl.ds(8, 8)
 
     def ring_copy(axis, kind):
         next_at, last_at = 1 + 2 * axis, 2 + 2 * axis
         up, down = device(HELD[next_at]), device(HELD[last_at])
+        far = (far_y, far_z)[axis]
         src, dst, target = {
             0: (held.at[0, low], held.at[last_at, low], up),
             1: (held.at[0, high], held.at[next_at, high], down),
             2: (held.at[0, high], held.at[last_at, high], up),
             3: (held.at[0, low], held.at[next_at, low], down),
-            4: (held.at[last_at, low], far.at[axis, low], up),
-            5: (held.at[next_at, high], far.at[axis, high], down),
+            4: (held.at[last_at, low], far.at[low], up),
+            5: (held.at[next_at, high], far.at[high], down),
         }[kind]
         return remote(src, dst, ring_send.at[axis, kind], ring_recv.at[axis, kind], target)
 
@@ -131,16 +142,24 @@
         for axis in range(2):
             ring[axis, kind].start()
 
-    def turn(n):
+    def turn(n, source, first=0, last=ROWS):
         def one(j, carry):
-            turned[n, j] = held[n, j].T
+            turned[n, j] = held[source, j].T
             return carry
 
-        lax.fori_loop(0, ROWS, one, 0)
-
-    turn(0)
+        lax.fori_loop(first, last, one, 0)
+
+    loads[5].wait()
+
+    def list_copy(k):
+        panel, worker = SENT[k]
+        worker = across if k == ACROSS else worker
+        return remote(blocks.at[at(panel)], blocks.at[PANELS + k], list_send.at[k], list_recv.at[k], device(worker))
+
+    list_copy(ACROSS).start()
+    turn(0, 0)
     for n in range(1, 6):
-        tab_copy(n, device(HELD[n])).wait_recv()
+        tab_copy(n, device(tab_targets[n - 1])).wait_recv()
     copies = [
         pltpu.make_async_copy(tab, tabs_s.at[0], tab_sem.at[0]),
         pltpu.make_async_copy(tabs.at[pl.ds(1, 5)], tabs_s.at[pl.ds(1, 5)], tab_sem.at[1]),
@@ -149,24 +168,20 @@
         copy.start()
     for copy in copies:
         copy.wait()
-    loads[5].wait()
 
     for kind in (0, 1):
         for axis in range(2):
             ring[axis, kind].wait_recv()
             ring[axis, kind + 4].start()
-
-    def list_copy(k):
-        panel, worker = SENT[k]
-        return remote(amat.at[at(panel)], listed.at[k], list_send.at[k], list_recv.at[k], device(worker))
-
-    for k in range(len(SENT)):
+    for k in range(ACROSS + 1, len(SENT)):
         list_copy(k).start()
+    for n, first in ((2, 0), (4, 0), (1, 8), (3, 8)):
+        turn(n, n, first, first + 8)
     for kind in (2, 3):
         for axis in range(2):
             ring[axis, kind].wait_recv()
-    for n in range(1, NEAR):
-        turn(n)
+    for n, first in ((2, 8), (4, 8), (1, 0), (3, 0)):
+        turn(n, n, first, first + 8)
 
     def gives(slot):
         return (
@@ -174,23 +189,20 @@
             remote(give.at[1, slot], got.at[1, slot], give_send.at[1, slot], got_recv.at[1, slot], above),
         )
 
-    def product(slot, blocks, lister, column, panel):
+    def product(slot, at_block, lister, column, panel):
+        entries = []
         for t in range(CAP):
-            span = pl.ds(t * PORES, PORES)
-            entry = held[column, tabs_s[lister, t, panel]]
-            mid[span, :] = jnp.dot(blocks[t], entry, preferred_element_type=F32).astype(BF16)
-            live = t < tabs_s[lister, T_COUNT, panel]
-            live = jnp.full((WIDTH, PORES), jnp.where(live, 1.0, 0.0), F32).astype(BF16)
-            lt[:, span] = turned[lister, tabs_s[lister, T_ROWS + t, panel]] * live
-        below_copy, above_copy = gives(slot)
-        for e, target in ((0, give.at[0, slot]), (2, give.at[1, slot]), (1, own.at[slot])):
-            target[...] = jnp.dot(
-                lt[pl.ds(e * PORES, PORES), :], mid[...], preferred_element_type=F32
-            ).astype(BF16)
-            if e == 0:
-                below_copy.start()
-            if e == 2:
-                above_copy.start()
+            live = jnp.where(t < tabs_s[lister, T_COUNT, panel], 1.0, 0.0)
+            block = blocks[at_block, t] * jnp.full((PORES, PORES), live, F32).astype(BF16)
+            row = turned[lister, tabs_s[lister, T_ROWS + t, panel]]
+            lt[:, pl.ds(t * PORES, PORES)] = jnp.dot(row, block, preferred_element_type=F32).astype(BF16)
+            entries.append(held[column, tabs_s[lister, t, panel]])
+        total = jnp.dot(lt[...], jnp.concatenate(entries, axis=0), preferred_element_type=F32).astype(BF16)
+        give[0, slot] = total[:PORES]
+        give[1, slot] = total[2 * PORES :]
+        own[slot] = total[PORES : 2 * PORES]
+        for copy in gives(slot):
+            copy.start()
 
     def summed(slot):
         for copy in gives(slot):
@@ -216,55 +228,73 @@
     def held_panel(i):
         return at((pick([p[0] for p in HELD], i), pick([p[1] for p in HELD], i)))
 
-    def local_step(i, carry):
-        panel = held_panel(i)
-        product(i, amat.at[panel], 0, i, panel)
-
-        @pl.when(i >= 2)
-        def _():
-            store(summed(i - 2), held_panel(i - 2))
-
-        return carry
-
     def back(k):
-        lister = (pick([HELD[n][0] for n in LISTER], k), pick([HELD[n][1] for n in LISTER], k))
+        far_one = pick(IS_ACROSS, k)
+        lister = tuple(
+            pick([HELD[n][axis] * (1 - a) for n, a in zip(LISTER, IS_ACROSS)], k) + far_one * across[axis]
+            for axis in range(2)
+        )
         return remote(result.at[k], returned.at[k], result_send.at[k], result_recv.at[k], device(lister))
 
-    def give_back(k):
-        for d, value in enumerate(summed(k + LOCAL)):
+    def give_back(k, slot):
+        for d, value in enumerate(summed(slot)):
             result[k, :, pl.ds(d * PORES, PORES)] = value.astype(BF16)
         back(k).start()
 
-    def sent_step(k, carry):
-        lister, column = pick(LISTER, k), pick(COLUMN, k)
+    def settle(axis):
+        for kind in (4, 5):
+            ring[axis, kind].wait_recv()
+        source = (far_y, far_z)[axis]
+
+        def one(j, carry):
+            held[NEAR + axis, j] = source[j]
+            return carry
+
+        lax.fori_loop(0, ROWS, one, 0)
+
+    def work(i, carry):
+        step = pick(ORDER, i)
+        here = pick([int(n < LOCAL) for n in ORDER], i)
+        k = (step - LOCAL) * (1 - here)
+        lister = pick(LISTER, k) * (1 - here)
+        column = step * here + (pick(COLUMN, k) - odd * pick(IS_ACROSS, k)) * (1 - here)
         panel = held_panel(column)
-        remote(listed.at[k], listed.at[k], list_send.at[k], list_recv.at[k], below).wait_recv()
-        product(k + LOCAL, listed.at[k], lister, column, panel)
-
-        @pl.when(k >= 2)
+
+        @pl.when(here == 0)
         def _():
-            give_back(k - 2)
-
-        return carry
-
-    lax.fori_loop(0, NEAR, local_step, 0)
-    for kind in (4, 5):
-        for axis in range(2):
-            ring[axis, kind].wait_recv()
-
-    def settle(j, carry):
-        for axis in range(2):
-            held[NEAR + axis, j] = far[axis, j]
-        return carry
-
-    lax.fori_loop(0, ROWS, settle, 0)
-    turn(NEAR)
-    lax.fori_loop(NEAR, LOCAL, local_step, 0)
-    for i in range(LOCAL - 2, LOCAL):
-        store(summed(i), held_panel(i))
+            remote(blocks.at[PANELS + k], blocks.at[PANELS + k], list_send.at[k], list_recv.at[k], below).wait_recv()
+
+        product(i, panel * here + (PANELS + k) * (1 - here), lister, column, panel)
+        return carry
+
+    def finish(i, carry):
+        step = pick(ORDER, i)
+
+        @pl.when(step < LOCAL)
+        def _():
+            store(summed(i), held_panel(step))
+
+        @pl.when(step >= LOCAL)
+        def _():
+            give_back(step - LOCAL, i)
+
+        return carry
+
+    def stretch(n, carry):
+        @pl.when(n == 1)
+        def _():
+            settle(0)
+            settle(1)
+            turn(NEAR, NEAR + odd)
+
+        first, last = pick(STARTS, n), pick(STARTS, n + 1)
+        lax.fori_loop(first, last, work, 0)
+        lax.fori_loop(first, last, finish, 0)
+        return carry
+
+    lax.fori_loop(0, len(STEPS), stretch, 0)
+
     last = len(SENT)
-    lax.fori_loop(0, last, sent_step, 0)
-    lax.fori_loop(last - 2, last, lambda k, carry: (give_back(k), carry)[1], 0)
 
     def arrive(k, carry):
         panel = at((pick([p[0] for p, _ in SENT], k), pick([p[1] for p, _ in SENT], k)))
@@ -275,7 +305,7 @@
     lax.fori_loop(0, last, arrive, 0)
 
     for n in range(1, 6):
-        tab_copy(n, device(minus((0, 0), HELD[n]))).wait_send()
+        tab_copy(n, device(tab_targets[n - 1])).wait_send()
     for copy in ring.values():
         copy.wait_send()
     for k in range(last):
@@ -294,23 +324,22 @@
         out_specs=pl.BlockSpec(memory_space=pltpu.VMEM),
         scratch_shapes=[
             pltpu.VMEM((ROWS, PORES, WIDTH), BF16),
-            pltpu.VMEM((PANELS, CAP, PORES, PORES), BF16),
+            pltpu.VMEM((PANELS + sent, CAP, PORES, PORES), BF16),
             pltpu.VMEM((LOCAL, ROWS, PORES, WIDTH), BF16),
-            pltpu.VMEM((2, ROWS, PORES, WIDTH), BF16),
+            pltpu.VMEM((ROWS, PORES, WIDTH), BF16),
+            pltpu.VMEM((ROWS, PORES, WIDTH), BF16),
             pltpu.VMEM((6, ROWS, WIDTH, PORES), BF16),
             pltpu.VMEM((T_ALL, PANELS), jnp.int32),
             pltpu.VMEM((6, T_ALL, PANELS), jnp.int32),
             pltpu.VMEM((1, PANELS), jnp.int32),
             pltpu.SMEM((3, 1, ROWS), jnp.int32),
             pltpu.SMEM((6, T_ALL, PANELS), jnp.int32),
-            pltpu.VMEM((sent, CAP, PORES, PORES), BF16),
             pltpu.VMEM((PANELS, PORES, WIDTH), BF16),
             pltpu.VMEM((2, PANELS, PORES, WIDTH), BF16),
             pltpu.VMEM((2, PANELS, PORES, WIDTH), BF16),
             pltpu.VMEM((sent, PORES, OFFSETS * PORES), BF16),
             pltpu.VMEM((sent, PORES, OFFSETS * PORES), BF16),
             pltpu.VMEM((WIDTH, CAP * PORES), BF16),
-            pltpu.VMEM((CAP * PORES, WIDTH), BF16),
             dma((6,)),
             dma((6,)),
             dma((6,)),

time: 101 us -> 94.5 us (0.936)
  Pallas kernels: 96.9 us -> 90.8 us
    pallas_call x1, Pallas kernels: 96.9 us -> 90.8 us  [per_device(): pl.pallas_call(kernel, out_shape=pltpu.VMEM((PORES * OFFSETS * PANELS, PO...]
where the time goes in v4:
time: 94.5 us; the launch traced here: 93.2 us
  Pallas kernels  90.8 us (96%)
  local copies, waits for them, and re-layouts  2.36 us (2%)
    pallas_call x1, Pallas kernels, per_device(): pl.pallas_call(kernel, out_shape=pltpu.VMEM((PORES * OFFSETS * PANELS, PO...  90.8 us
    unnamed x1, local copies, waits for them, and re-layouts  2.36 us

profile of v4, /device:TPU:1, one launch (start us, length us, event | category | flops | bytes accessed | tf_op | source)
XLA Modules:
  0.0 93.2 jit_solution(8177627861742028522)
XLA Ops:
  0.0 90.8 %shard_map.64 = f32[10240,128]{1,0:T(8,128)S(1)} custom-call(bf16[16,8,128,128]{3,2,1,0:T(8,128)(2,1)} %bitcast.16, bf16[16,128,384]{2,1,0:T(8,128)(2,1)} %bitcast.17, s32[8,16]{1,0:T(8,128)} %bitcast.18, s32[8,16]{1,0:T(8,128)} %bitcast.19, s32[1,16]{1,0:T(1,128)} %bitcast.21, s32[3,1,16]{2,1,0:T(1,128)} %bitcast.20), custom_call_target="tpu_custom_call" | custom-call | flops 6499999744 | bytes 12000000 | tf_op jit(solution)/shard_map/pallas_call | solution.py:320
  90.9 2.4 %copy.8 = f32[1,1,128,16,5,128]{5,3,4,2,1,0:T(8,128)} copy(f32[1,1,128,16,5,128]{5,3,4,2,1,0:T(8,128)S(1)} %bitcast.15) | data formatting | bytes 10485760

commit v5 on v4

--- a/solution.py
+++ b/solution.py
@@ -20,11 +20,11 @@
 HELD = ((0, 0), (0, 1), (0, 3), (1, 0), (3, 0), (0, 2), (2, 0))
 NEAR, LOCAL = 5, 7
 SENT = (
-    ((2, 2), (0, 2)),
+    ((2, 2), (0, 2)), ((1, 1), (1, 0)), ((3, 3), (3, 0)),
     ((2, 1), (0, 1)), ((2, 3), (0, 3)), ((1, 2), (1, 0)), ((3, 2), (3, 0)),
-    ((3, 1), (0, 1)), ((1, 3), (0, 3)), ((1, 1), (1, 0)), ((3, 3), (3, 0)),
+    ((1, 3), (0, 3)), ((3, 1), (3, 0)),
 )
-ACROSS = 0
+FIRST = 3
 
 
 def minus(p, q):
@@ -33,33 +33,42 @@
 
 LISTER = tuple(HELD.index(minus((0, 0), h)) for _, h in SENT)
 COLUMN = tuple(HELD.index(minus(p, h)) for p, h in SENT)
-IS_ACROSS = tuple(int(k == ACROSS) for k in range(len(SENT)))
-STEPS = ((0, 1, 2, 3, 4), (7, 5, 6, 8, 9, 10, 11), (12, 13, 14, 15))
-ORDER = sum(STEPS, ())
-STARTS = tuple(sum(len(s) for s in STEPS[:n]) for n in range(len(STEPS) + 1))
+PRODUCT, SUM, RETURN, TURN = range(4)
+ORDER = (
+    *((PRODUCT, i) for i in (0, 1, 2, 3, 4, 8, 9)),
+    *((SUM, i) for i in (0, 1, 2, 3, 4, 8, 9)),
+    (PRODUCT, 5), (PRODUCT, 6), (TURN, 5), (PRODUCT, 7),
+    *((PRODUCT, i) for i in (10, 11, 12, 13)),
+    *((SUM, i) for i in (7, 5, 6, 10, 11)),
+    (PRODUCT, 14), (PRODUCT, 15),
+    *((SUM, i) for i in (12, 13, 14, 15)),
+    *((RETURN, k) for k in (1, 2, 0, 3, 4, 5, 6, 7, 8)),
+)
+FAR_OP = ORDER.index((PRODUCT, 5))
 
 
 def pick(values, i):
     if isinstance(i, int):
         return values[i]
-    total = values[0]
-    for k in range(1, len(values)):
-        if values[k] != values[k - 1]:
-            total = total + (values[k] - values[k - 1]) * (i >= k).astype(jnp.int32)
-    return total
+    words = []
+    for first in range(0, len(values), 8):
+        word = sum(value << (4 * n) for n, value in enumerate(values[first : first + 8]))
+        words.append(word - (1 << 32) if word >= 1 << 31 else word)
+    chosen = jnp.int32(words[-1])
+    for n in range(len(words) - 2, -1, -1):
+        chosen = jnp.where(i < 8 * (n + 1), jnp.int32(words[n]), chosen)
+    return lax.shift_right_logical(chosen, (i & 7) * 4) & 15
 
 
 def kernel(
     fine, prolong, cols_h, rows_h, counts_h, mask_h, out,
-    stage, blocks, held, far_y, far_z, turned, tab, tabs, counts, mask, tabs_s,
-    own, give, got, result, returned, lt,
+    stage, blocks, held, far, turned, tab, tabs, counts, mask, tabs_s,
+    own, give, got, result, returned, mid,
     load_sem, tab_send, tab_recv, tab_sem, ring_send, ring_recv, list_send, list_recv, give_send, got_recv,
     result_send, result_recv,
 ):
     blk, g = lax.axis_index("blk"), lax.axis_index("rows")
     z, y = blk // SIDE, blk % SIDE
-    odd = (z + y) % 2
-    across = (2 * odd, 2 * (1 - odd))
 
     def at(offset):
         dz, dy = offset
@@ -71,7 +80,7 @@
     below, above = (blk, (g + GROUPS - 1) % GROUPS), (blk, (g + 1) % GROUPS)
 
     barrier = pltpu.get_barrier_semaphore()
-    friends = [device(offset) for offset in HELD[1:NEAR] + (across,)] + [below, above]
+    friends = [device(offset) for offset in HELD[1:6]] + [below, above]
     for friend in friends:
         pl.semaphore_signal(barrier, inc=1, device_id=friend, device_id_type=MESH)
 
@@ -117,7 +126,7 @@
     def tab_copy(n, target):
         return remote(tab, tabs.at[n], tab_send.at[n], tab_recv.at[n], target)
 
-    tab_targets = [minus((0, 0), HELD[n]) for n in range(1, NEAR)] + [across]
+    tab_targets = [minus((0, 0), HELD[n]) for n in range(1, 6)]
     for n in range(1, 6):
         tab_copy(n, device(tab_targets[n - 1])).start()
 
@@ -126,14 +135,13 @@
     def ring_copy(axis, kind):
         next_at, last_at = 1 + 2 * axis, 2 + 2 * axis
         up, down = device(HELD[next_at]), device(HELD[last_at])
-        far = (far_y, far_z)[axis]
         src, dst, target = {
             0: (held.at[0, low], held.at[last_at, low], up),
             1: (held.at[0, high], held.at[next_at, high], down),
             2: (held.at[0, high], held.at[last_at, high], up),
             3: (held.at[0, low], held.at[next_at, low], down),
-            4: (held.at[last_at, low], far.at[low], up),
-            5: (held.at[next_at, high], far.at[high], down),
+            4: (held.at[last_at, low], far.at[axis, low], up),
+            5: (held.at[next_at, high], far.at[axis, high], down),
         }[kind]
         return remote(src, dst, ring_send.at[axis, kind], ring_recv.at[axis, kind], target)
 
@@ -142,9 +150,9 @@
         for axis in range(2):
             ring[axis, kind].start()
 
-    def turn(n, source, first=0, last=ROWS):
+    def turn(n, first=0, last=ROWS):
         def one(j, carry):
-            turned[n, j] = held[source, j].T
+            turned[n, j] = (held[n, j] if n < NEAR else far[n - NEAR, j]).T
             return carry
 
         lax.fori_loop(first, last, one, 0)
@@ -153,11 +161,11 @@
 
     def list_copy(k):
         panel, worker = SENT[k]
-        worker = across if k == ACROSS else worker
         return remote(blocks.at[at(panel)], blocks.at[PANELS + k], list_send.at[k], list_recv.at[k], device(worker))
 
-    list_copy(ACROSS).start()
-    turn(0, 0)
+    for k in range(FIRST):
+        list_copy(k).start()
+    turn(0)
     for n in range(1, 6):
         tab_copy(n, device(tab_targets[n - 1])).wait_recv()
     copies = [
@@ -173,15 +181,15 @@
         for axis in range(2):
             ring[axis, kind].wait_recv()
             ring[axis, kind + 4].start()
-    for k in range(ACROSS + 1, len(SENT)):
+    for k in range(FIRST, len(SENT)):
         list_copy(k).start()
     for n, first in ((2, 0), (4, 0), (1, 8), (3, 8)):
-        turn(n, n, first, first + 8)
+        turn(n, first, first + 8)
     for kind in (2, 3):
         for axis in range(2):
             ring[axis, kind].wait_recv()
     for n, first in ((2, 8), (4, 8), (1, 0), (3, 0)):
-        turn(n, n, first, first + 8)
+        turn(n, first, first + 8)
 
     def gives(slot):
         return (
@@ -189,15 +197,15 @@
             remote(give.at[1, slot], got.at[1, slot], give_send.at[1, slot], got_recv.at[1, slot], above),
         )
 
-    def product(slot, at_block, lister, column, panel):
-        entries = []
+    def product(source, slot, at_block, lister, column, panel):
+        rows = []
         for t in range(CAP):
             live = jnp.where(t < tabs_s[lister, T_COUNT, panel], 1.0, 0.0)
             block = blocks[at_block, t] * jnp.full((PORES, PORES), live, F32).astype(BF16)
-            row = turned[lister, tabs_s[lister, T_ROWS + t, panel]]
-            lt[:, pl.ds(t * PORES, PORES)] = jnp.dot(row, block, preferred_element_type=F32).astype(BF16)
-            entries.append(held[column, tabs_s[lister, t, panel]])
-        total = jnp.dot(lt[...], jnp.concatenate(entries, axis=0), preferred_element_type=F32).astype(BF16)
+            entry = source[column, tabs_s[lister, t, panel]]
+            mid[pl.ds(t * PORES, PORES), :] = jnp.dot(block, entry, preferred_element_type=F32).astype(BF16)
+            rows.append(turned[lister, tabs_s[lister, T_ROWS + t, panel]])
+        total = jnp.dot(jnp.concatenate(rows, axis=1), mid[...], preferred_element_type=F32).astype(BF16)
         give[0, slot] = total[:PORES]
         give[1, slot] = total[2 * PORES :]
         own[slot] = total[PORES : 2 * PORES]
@@ -229,11 +237,7 @@
         return at((pick([p[0] for p in HELD], i), pick([p[1] for p in HELD], i)))
 
     def back(k):
-        far_one = pick(IS_ACROSS, k)
-        lister = tuple(
-            pick([HELD[n][axis] * (1 - a) for n, a in zip(LISTER, IS_ACROSS)], k) + far_one * across[axis]
-            for axis in range(2)
-        )
+        lister = (pick([HELD[n][0] for n in LISTER], k), pick([HELD[n][1] for n in LISTER], k))
         return remote(result.at[k], returned.at[k], result_send.at[k], result_recv.at[k], device(lister))
 
     def give_back(k, slot):
@@ -241,68 +245,68 @@
             result[k, :, pl.ds(d * PORES, PORES)] = value.astype(BF16)
         back(k).start()
 
-    def settle(axis):
-        for kind in (4, 5):
-            ring[axis, kind].wait_recv()
-        source = (far_y, far_z)[axis]
-
-        def one(j, carry):
-            held[NEAR + axis, j] = source[j]
-            return carry
-
-        lax.fori_loop(0, ROWS, one, 0)
-
-    def work(i, carry):
-        step = pick(ORDER, i)
-        here = pick([int(n < LOCAL) for n in ORDER], i)
-        k = (step - LOCAL) * (1 - here)
+    def work(i):
+        here = (i < LOCAL).astype(jnp.int32)
+        k = (i - LOCAL) * (1 - here)
         lister = pick(LISTER, k) * (1 - here)
-        column = step * here + (pick(COLUMN, k) - odd * pick(IS_ACROSS, k)) * (1 - here)
+        column = i * here + pick(COLUMN, k) * (1 - here)
         panel = held_panel(column)
+        at_block = panel * here + (PANELS + k) * (1 - here)
 
         @pl.when(here == 0)
         def _():
             remote(blocks.at[PANELS + k], blocks.at[PANELS + k], list_send.at[k], list_recv.at[k], below).wait_recv()
 
-        product(i, panel * here + (PANELS + k) * (1 - here), lister, column, panel)
-        return carry
-
-    def finish(i, carry):
-        step = pick(ORDER, i)
-
-        @pl.when(step < LOCAL)
-        def _():
-            store(summed(i), held_panel(step))
-
-        @pl.when(step >= LOCAL)
-        def _():
-            give_back(step - LOCAL, i)
-
-        return carry
-
-    def stretch(n, carry):
-        @pl.when(n == 1)
-        def _():
-            settle(0)
-            settle(1)
-            turn(NEAR, NEAR + odd)
-
-        first, last = pick(STARTS, n), pick(STARTS, n + 1)
-        lax.fori_loop(first, last, work, 0)
-        lax.fori_loop(first, last, finish, 0)
-        return carry
-
-    lax.fori_loop(0, len(STEPS), stretch, 0)
-
-    last = len(SENT)
-
-    def arrive(k, carry):
+        @pl.when(column < NEAR)
+        def _():
+            product(held, i, at_block, lister, column, panel)
+
+        @pl.when(column >= NEAR)
+        def _():
+            product(far, i, at_block, lister, column - NEAR, panel)
+
+    def finish(i):
+        @pl.when(i < LOCAL)
+        def _():
+            store(summed(i), held_panel(i))
+
+        @pl.when(i >= LOCAL)
+        def _():
+            give_back(i - LOCAL, i)
+
+    def arrive(k):
         panel = at((pick([p[0] for p, _ in SENT], k), pick([p[1] for p, _ in SENT], k)))
         back(k).wait_recv()
         store([returned[k, :, pl.ds(d * PORES, PORES)].astype(F32) for d in range(OFFSETS)], panel)
+
+    def operate(n, carry):
+        kind, i = pick([op for op, _ in ORDER], n), pick([i for _, i in ORDER], n)
+
+        @pl.when(kind == PRODUCT)
+        def _():
+            work(i)
+
+        @pl.when(kind == SUM)
+        def _():
+            finish(i)
+
+        @pl.when(kind == RETURN)
+        def _():
+            arrive(i)
+
+        @pl.when(kind == TURN)
+        def _():
+            turn(NEAR)
+
         return carry
 
-    lax.fori_loop(0, last, arrive, 0)
+    lax.fori_loop(0, FAR_OP, operate, 0)
+    for kind in (4, 5):
+        for axis in range(2):
+            ring[axis, kind].wait_recv()
+    lax.fori_loop(FAR_OP, len(ORDER), operate, 0)
+
+    last = len(SENT)
 
     for n in range(1, 6):
         tab_copy(n, device(tab_targets[n - 1])).wait_send()
@@ -325,9 +329,8 @@
         scratch_shapes=[
             pltpu.VMEM((ROWS, PORES, WIDTH), BF16),
             pltpu.VMEM((PANELS + sent, CAP, PORES, PORES), BF16),
-            pltpu.VMEM((LOCAL, ROWS, PORES, WIDTH), BF16),
-            pltpu.VMEM((ROWS, PORES, WIDTH), BF16),
-            pltpu.VMEM((ROWS, PORES, WIDTH), BF16),
+            pltpu.VMEM((NEAR, ROWS, PORES, WIDTH), BF16),
+            pltpu.VMEM((2, ROWS, PORES, WIDTH), BF16),
             pltpu.VMEM((6, ROWS, WIDTH, PORES), BF16),
             pltpu.VMEM((T_ALL, PANELS), jnp.int32),
             pltpu.VMEM((6, T_ALL, PANELS), jnp.int32),
@@ -339,7 +342,7 @@
             pltpu.VMEM((2, PANELS, PORES, WIDTH), BF16),
             pltpu.VMEM((sent, PORES, OFFSETS * PORES), BF16),
             pltpu.VMEM((sent, PORES, OFFSETS * PORES), BF16),
-            pltpu.VMEM((WIDTH, CAP * PORES), BF16),
+            pltpu.VMEM((CAP * PORES, WIDTH), BF16),
             dma((6,)),
             dma((6,)),
             dma((6,)),

time: 94.5 us -> 92.3 us (0.977); the launches traced: 93.2 us -> 92.2 us
  Pallas kernels: 90.8 us -> 89.8 us
    pallas_call x1, Pallas kernels: 90.8 us -> 89.8 us  [per_device(): pl.pallas_call(kernel, out_shape=pltpu.VMEM((PORES * OFFSETS * PANELS, PO...]
where the time goes in v5:
time: 92.3 us; the launch traced here: 92.2 us
  Pallas kernels  89.8 us (97%)
  local copies, waits for them, and re-layouts  2.36 us (3%)
    pallas_call x1, Pallas kernels, per_device(): pl.pallas_call(kernel, out_shape=pltpu.VMEM((PORES * OFFSETS * PANELS, PO...  89.8 us
    unnamed x1, local copies, waits for them, and re-layouts  2.36 us

profile of v5, /device:TPU:1, one launch (start us, length us, event | category | flops | bytes accessed | tf_op | source)
XLA Modules:
  0.0 92.2 jit_solution(8696675478177111557)
XLA Ops:
  0.0 89.8 %shard_map.64 = f32[10240,128]{1,0:T(8,128)S(1)} custom-call(bf16[16,8,128,128]{3,2,1,0:T(8,128)(2,1)} %bitcast.16, bf16[16,128,384]{2,1,0:T(8,128)(2,1)} %bitcast.17, s32[8,16]{1,0:T(8,128)} %bitcast.18, s32[8,16]{1,0:T(8,128)} %bitcast.19, s32[1,16]{1,0:T(1,128)} %bitcast.21, s32[3,1,16]{2,1,0:T(1,128)} %bitcast.20), custom_call_target="tpu_custom_call" | custom-call | flops 6499999744 | bytes 12000000 | tf_op jit(solution)/shard_map/pallas_call | solution.py:324
  89.8 2.4 %copy.8 = f32[1,1,128,16,5,128]{5,3,4,2,1,0:T(8,128)} copy(f32[1,1,128,16,5,128]{5,3,4,2,1,0:T(8,128)S(1)} %bitcast.15) | data formatting | bytes 10485760

commit v6 on v5

--- a/solution.py
+++ b/solution.py
@@ -10,6 +10,7 @@
 F32 = jnp.float32
 SIDE = 4
 ROWS = 16
+UP = (10, 9)
 CAP = 8
 PORES = 128
 WIDTH = 384
@@ -20,11 +21,17 @@
 HELD = ((0, 0), (0, 1), (0, 3), (1, 0), (3, 0), (0, 2), (2, 0))
 NEAR, LOCAL = 5, 7
 SENT = (
-    ((2, 2), (0, 2)), ((1, 1), (1, 0)), ((3, 3), (3, 0)),
-    ((2, 1), (0, 1)), ((2, 3), (0, 3)), ((1, 2), (1, 0)), ((3, 2), (3, 0)),
-    ((1, 3), (0, 3)), ((3, 1), (3, 0)),
+    ((2, 2), (0, 2)),
+    ((1, 1), (1, 0)),
+    ((3, 3), (3, 0)),
+    ((1, 3), (0, 3)),
+    ((3, 1), (3, 0)),
+    ((2, 1), (0, 1)),
+    ((2, 3), (0, 3)),
+    ((1, 2), (1, 0)),
+    ((3, 2), (3, 0)),
 )
-FIRST = 3
+FIRST = 5
 
 
 def minus(p, q):
@@ -35,14 +42,40 @@
 COLUMN = tuple(HELD.index(minus(p, h)) for p, h in SENT)
 PRODUCT, SUM, RETURN, TURN = range(4)
 ORDER = (
-    *((PRODUCT, i) for i in (0, 1, 2, 3, 4, 8, 9)),
-    *((SUM, i) for i in (0, 1, 2, 3, 4, 8, 9)),
-    (PRODUCT, 5), (PRODUCT, 6), (TURN, 5), (PRODUCT, 7),
-    *((PRODUCT, i) for i in (10, 11, 12, 13)),
-    *((SUM, i) for i in (7, 5, 6, 10, 11)),
-    (PRODUCT, 14), (PRODUCT, 15),
-    *((SUM, i) for i in (12, 13, 14, 15)),
-    *((RETURN, k) for k in (1, 2, 0, 3, 4, 5, 6, 7, 8)),
+    (PRODUCT, 0),
+    (PRODUCT, 1),
+    (PRODUCT, 2),
+    (PRODUCT, 3),
+    (PRODUCT, 4),
+    (PRODUCT, 8),
+    (PRODUCT, 9),
+    (PRODUCT, 10),
+    (PRODUCT, 11),
+    (SUM, 0),
+    (SUM, 1),
+    (SUM, 2),
+    (SUM, 3),
+    (SUM, 4),
+    (SUM, 8),
+    (SUM, 9),
+    (SUM, 10),
+    (SUM, 11),
+    (PRODUCT, 5),
+    (TURN, 5),
+    (PRODUCT, 7),
+    (PRODUCT, 6),
+    (PRODUCT, 13),
+    (PRODUCT, 15),
+    (PRODUCT, 12),
+    (PRODUCT, 14),
+    (SUM, 7),
+    (SUM, 5),
+    (SUM, 6),
+    (SUM, 13),
+    (SUM, 15),
+    (SUM, 12),
+    (SUM, 14),
+    *((RETURN, k) for k in (0, 1, 2, 3, 4, 6, 8, 5, 7)),
 )
 FAR_OP = ORDER.index((PRODUCT, 5))
 
@@ -130,10 +163,10 @@
     for n in range(1, 6):
         tab_copy(n, device(tab_targets[n - 1])).start()
 
-    low, high = pl.ds(0, 8), pl.ds(8, 8)
 
     def ring_copy(axis, kind):
         next_at, last_at = 1 + 2 * axis, 2 + 2 * axis
+        low, high = pl.ds(0, UP[axis]), pl.ds(UP[axis], ROWS - UP[axis])
         up, down = device(HELD[next_at]), device(HELD[last_at])
         src, dst, target = {
             0: (held.at[0, low], held.at[last_at, low], up),
@@ -183,13 +216,14 @@
             ring[axis, kind + 4].start()
     for k in range(FIRST, len(SENT)):
         list_copy(k).start()
-    for n, first in ((2, 0), (4, 0), (1, 8), (3, 8)):
-        turn(n, first, first + 8)
+    up_y, up_z = UP
+    for n, first, last in ((2, 0, up_y), (4, 0, up_z), (1, up_y, ROWS), (3, up_z, ROWS)):
+        turn(n, first, last)
     for kind in (2, 3):
         for axis in range(2):
             ring[axis, kind].wait_recv()
-    for n, first in ((2, 8), (4, 8), (1, 0), (3, 0)):
-        turn(n, first, first + 8)
+    for n, first, last in ((2, up_y, ROWS), (4, up_z, ROWS), (1, 0, up_y), (3, 0, up_z)):
+        turn(n, first, last)
 
     def gives(slot):
         return (

time: 92.3 us -> 91.2 us (0.988)
  Pallas kernels: 89.8 us -> 88.7 us
    pallas_call x1, Pallas kernels: 89.8 us -> 88.7 us  [per_device(): pl.pallas_call(kernel, out_shape=pltpu.VMEM((PORES * OFFSETS * PANELS, PO...]
where the time goes in v6:
time: 91.2 us; the launch traced here: 91.1 us
  Pallas kernels  88.7 us (97%)
  local copies, waits for them, and re-layouts  2.36 us (3%)
    pallas_call x1, Pallas kernels, per_device(): pl.pallas_call(kernel, out_shape=pltpu.VMEM((PORES * OFFSETS * PANELS, PO...  88.7 us
    unnamed x1, local copies, waits for them, and re-layouts  2.36 us

profile of v6, /device:TPU:1, one launch (start us, length us, event | category | flops | bytes accessed | tf_op | source)
XLA Modules:
  0.0 91.1 jit_solution(11224686652439151122)
XLA Ops:
  0.0 88.7 %shard_map.64 = f32[10240,128]{1,0:T(8,128)S(1)} custom-call(bf16[16,8,128,128]{3,2,1,0:T(8,128)(2,1)} %bitcast.16, bf16[16,128,384]{2,1,0:T(8,128)(2,1)} %bitcast.17, s32[8,16]{1,0:T(8,128)} %bitcast.18, s32[8,16]{1,0:T(8,128)} %bitcast.19, s32[1,16]{1,0:T(1,128)} %bitcast.21, s32[3,1,16]{2,1,0:T(1,128)} %bitcast.20), custom_call_target="tpu_custom_call" | custom-call | flops 6499999744 | bytes 12000000 | tf_op jit(solution)/shard_map/pallas_call | solution.py:358
  88.7 2.4 %copy.8 = f32[1,1,128,16,5,128]{5,3,4,2,1,0:T(8,128)} copy(f32[1,1,128,16,5,128]{5,3,4,2,1,0:T(8,128)S(1)} %bitcast.15) | data formatting | bytes 10485760

commit v7 on v6

--- a/solution.py
+++ b/solution.py
@@ -10,6 +10,7 @@
 F32 = jnp.float32
 SIDE = 4
 ROWS = 16
+SPLIT = 10
 UP = (10, 9)
 CAP = 8
 PORES = 128
@@ -60,24 +61,24 @@
     (SUM, 9),
     (SUM, 10),
     (SUM, 11),
-    (PRODUCT, 5),
     (TURN, 5),
     (PRODUCT, 7),
-    (PRODUCT, 6),
     (PRODUCT, 13),
     (PRODUCT, 15),
     (PRODUCT, 12),
     (PRODUCT, 14),
     (SUM, 7),
-    (SUM, 5),
-    (SUM, 6),
+    (PRODUCT, 5),
+    (PRODUCT, 6),
     (SUM, 13),
     (SUM, 15),
     (SUM, 12),
     (SUM, 14),
+    (SUM, 5),
+    (SUM, 6),
     *((RETURN, k) for k in (0, 1, 2, 3, 4, 6, 8, 5, 7)),
 )
-FAR_OP = ORDER.index((PRODUCT, 5))
+FAR_OP = ORDER.index((TURN, 5))
 
 
 def pick(values, i):
@@ -121,8 +122,9 @@
         pltpu.make_async_copy(src, dst, load_sem.at[n])
         for n, (src, dst) in enumerate(
             (
-                (prolong, stage),
                 (mask_h, mask),
+                (prolong.at[pl.ds(0, SPLIT)], stage.at[pl.ds(0, SPLIT)]),
+                (prolong.at[pl.ds(SPLIT, ROWS - SPLIT)], stage.at[pl.ds(SPLIT, ROWS - SPLIT)]),
                 (cols_h, tab.at[pl.ds(0, CAP)]),
                 (rows_h, tab.at[pl.ds(T_ROWS, CAP)]),
                 (counts_h, counts),
@@ -130,16 +132,13 @@
             )
         )
     ]
-    for load in loads:
+    for load in loads[:6]:
         load.start()
 
     def remote(src, dst, send, recv, target):
         return pltpu.make_async_remote_copy(
             src_ref=src, dst_ref=dst, send_sem=send, recv_sem=recv, device_id=target, device_id_type=MESH
         )
-
-    for load in loads[:2]:
-        load.wait()
 
     def mask_row(j, carry):
         for e in range(3):
@@ -150,8 +149,13 @@
             held[0, j, :, span] = stage[j, :, span] * keep
         return carry
 
-    lax.fori_loop(0, ROWS, mask_row, 0)
-    for load in loads[2:5]:
+    for load in loads[:2]:
+        load.wait()
+    lax.fori_loop(0, SPLIT, mask_row, 0)
+    loads[2].wait()
+    loads[6].start()
+    lax.fori_loop(SPLIT, ROWS, mask_row, 0)
+    for load in loads[3:6]:
         load.wait()
     tab[pl.ds(T_COUNT, CAP), :] = jnp.broadcast_to(counts[...], (CAP, PANELS))
     pl.semaphore_wait(barrier, len(friends))
@@ -190,7 +194,7 @@
 
         lax.fori_loop(first, last, one, 0)
 
-    loads[5].wait()
+    loads[6].wait()
 
     def list_copy(k):
         panel, worker = SENT[k]
@@ -377,7 +381,7 @@
             pltpu.VMEM((sent, PORES, OFFSETS * PORES), BF16),
             pltpu.VMEM((sent, PORES, OFFSETS * PORES), BF16),
             pltpu.VMEM((CAP * PORES, WIDTH), BF16),
-            dma((6,)),
+            dma((7,)),
             dma((6,)),
             dma((6,)),
             dma((2,)),

time: 91.2 us -> 90 us (0.987)
  Pallas kernels: 88.7 us -> 87.5 us
    pallas_call x1, Pallas kernels: 88.7 us -> 87.5 us  [per_device(): pl.pallas_call(kernel, out_shape=pltpu.VMEM((PORES * OFFSETS * PANELS, PO...]
where the time goes in v7:
time: 90 us; the launch traced here: 89.9 us
  Pallas kernels  87.5 us (97%)
  local copies, waits for them, and re-layouts  2.36 us (3%)
    pallas_call x1, Pallas kernels, per_device(): pl.pallas_call(kernel, out_shape=pltpu.VMEM((PORES * OFFSETS * PANELS, PO...  87.5 us
    unnamed x1, local copies, waits for them, and re-layouts  2.36 us

profile of v7, /device:TPU:1, one launch (start us, length us, event | category | flops | bytes accessed | tf_op | source)
XLA Modules:
  0.0 89.9 jit_solution(2297783385957503676)
XLA Ops:
  0.0 87.5 %shard_map.64 = f32[10240,128]{1,0:T(8,128)S(1)} custom-call(bf16[16,8,128,128]{3,2,1,0:T(8,128)(2,1)} %bitcast.16, bf16[16,128,384]{2,1,0:T(8,128)(2,1)} %bitcast.17, s32[8,16]{1,0:T(8,128)} %bitcast.18, s32[8,16]{1,0:T(8,128)} %bitcast.19, s32[1,16]{1,0:T(1,128)} %bitcast.21, s32[3,1,16]{2,1,0:T(1,128)} %bitcast.20), custom_call_target="tpu_custom_call" | custom-call | flops 6499999744 | bytes 12000000 | tf_op jit(solution)/shard_map/pallas_call | solution.py:362
  87.5 2.4 %copy.8 = f32[1,1,128,16,5,128]{5,3,4,2,1,0:T(8,128)} copy(f32[1,1,128,16,5,128]{5,3,4,2,1,0:T(8,128)S(1)} %bitcast.15) | data formatting | bytes 10485760

commit v8 on v7

--- a/solution.py
+++ b/solution.py
@@ -68,14 +68,8 @@
     (PRODUCT, 12),
     (PRODUCT, 14),
     (SUM, 7),
-    (PRODUCT, 5),
-    (PRODUCT, 6),
-    (SUM, 13),
-    (SUM, 15),
-    (SUM, 12),
-    (SUM, 14),
-    (SUM, 5),
-    (SUM, 6),
+    (PRODUCT, 5), (SUM, 13), (PRODUCT, 6), (SUM, 15), (SUM, 12), (SUM, 14),
+    (SUM, 5), (SUM, 6),
     *((RETURN, k) for k in (0, 1, 2, 3, 4, 6, 8, 5, 7)),
 )
 FAR_OP = ORDER.index((TURN, 5))

time: 90 us -> 90.4 us (level)
  no operation moved by 1% of the time
where the time goes in v8:
time: 90.4 us; the launch traced here: 90.3 us
  Pallas kernels  87.9 us (97%)
  local copies, waits for them, and re-layouts  2.36 us (3%)
    pallas_call x1, Pallas kernels, per_device(): pl.pallas_call(kernel, out_shape=pltpu.VMEM((PORES * OFFSETS * PANELS, PO...  87.9 us
    unnamed x1, local copies, waits for them, and re-layouts  2.36 us

profile of v8, /device:TPU:1, one launch (start us, length us, event | category | flops | bytes accessed | tf_op | source)
XLA Modules:
  0.0 90.3 jit_solution(14572270527251058667)
XLA Ops:
  0.0 87.9 %shard_map.64 = f32[10240,128]{1,0:T(8,128)S(1)} custom-call(bf16[16,8,128,128]{3,2,1,0:T(8,128)(2,1)} %bitcast.16, bf16[16,128,384]{2,1,0:T(8,128)(2,1)} %bitcast.17, s32[8,16]{1,0:T(8,128)} %bitcast.18, s32[8,16]{1,0:T(8,128)} %bitcast.19, s32[1,16]{1,0:T(1,128)} %bitcast.21, s32[3,1,16]{2,1,0:T(1,128)} %bitcast.20), custom_call_target="tpu_custom_call" | custom-call | flops 6499999744 | bytes 12000000 | tf_op jit(solution)/shard_map/pallas_call | solution.py:356
  87.9 2.4 %copy.8 = f32[1,1,128,16,5,128]{5,3,4,2,1,0:T(8,128)} copy(f32[1,1,128,16,5,128]{5,3,4,2,1,0:T(8,128)S(1)} %bitcast.15) | data formatting | bytes 10485760
